TPU v7x, 128 devices: a whole 4x4x4 slice. The times are simulated.
128 devices in a mesh: gx: 8 (over z, core), gy: 16 (over y, x).
Axes of the slice: x: 4, y: 4, z: 4, core: 2. Of those that a mesh axis runs over, the one named last changes fastest.
Arguments:
- fields: bfloat16 [2, 16, 128, 2048], P(None, None, 'gx', 'gy'), may hold values from -6 to 6
- phase: int32 [128, 2048], P('gx', 'gy'), may hold values 0 or 1
- electrode: int32 [2, 128, 2048], P(None, 'gx', 'gy'), may hold values 0 or 1
- planes: float32 [2, 2, 16, 32, 2048], P(None, None, None, 'gx', 'gy'), may hold values from -6 to 6
Outputs:
- new_fields: float32 [2, 16, 128, 2048], P(None, None, 'gx', 'gy')
- new_planes: float32 [2, 2, 16, 32, 2048], P(None, None, None, 'gx', 'gy')
All inputs are finite; a program needn't handle non-finite values. No bound on the sum of `phase` or of `electrode` on one device may be relied on, other than what follows from the above.
Results may differ from a plain program's by a relative error of at most 0.00035.
Values sent between devices are 32-bit elements; how exact they have to be, the bound alone decides.
A program may use at most 64 MiB of HBM per device.

v0:
```python
import jax
import jax.numpy as jnp
from jax import lax
from jax.sharding import PartitionSpec as P

cond_oil = 0.6
cond_drop = 2.0
diff_oil = 0.3
diff_drop = 1.0
thermal_slope = 0.3
joule_rate = 0.5
time_step = 2.0
robin_weight = 2.0
extrap_half = 0.5
cheb_centre = 1.0
cheb_radius = 0.95
cheb_ratio = cheb_centre / cheb_radius
rho_first = 1.0 / cheb_ratio
rho_second = 1.0 / (2.0 * cheb_ratio - rho_first)


def padded_2(cells, sides, width):
    for axis, dim in sides:
        count = lax.axis_size(axis)
        ends = count - 1
        head = lax.slice_in_dim(cells, 0, width, axis=dim)
        tail = lax.slice_in_dim(cells, cells.shape[dim] - width, cells.shape[dim], axis=dim)
        cells = jnp.concatenate(
            [
                lax.ppermute(tail, axis, [(i, (i + 1) % count) for i in range(ends)]),
                cells,
                lax.ppermute(head, axis, [((i + 1) % count, i) for i in range(ends)]),
            ],
            axis=dim,
        )
    return cells


def shift_pad(values, axis, before, after):
    widths = [(0, 0)] * values.ndim
    widths[axis] = (before, after)
    return jnp.pad(values, widths)


def couple(padded, conduct, faces):
    centre = padded[..., 1:-1]
    middle = conduct[..., 1:-1]
    vertical = 0.5 * (middle[:, 1:] + middle[:, :-1])
    vert_flux = vertical * (centre[:, 1:] - centre[:, :-1])
    leakage = shift_pad(-vert_flux, 1, 0, 1) + shift_pad(vert_flux, 1, 1, 0)
    spread = shift_pad(vertical, 1, 0, 1) + shift_pad(vertical, 1, 1, 0)
    along = 0.5 * (middle[:, :, 1:] + middle[:, :, :-1])
    along_flux = along * (centre[:, :, 1:] - centre[:, :, :-1])
    leakage = leakage + shift_pad(-along_flux, 2, 0, 1) + shift_pad(along_flux, 2, 1, 0)
    spread = spread + shift_pad(along, 2, 0, 1) + shift_pad(along, 2, 1, 0)
    across = 0.5 * (conduct[..., 1:] + conduct[..., :-1]) * faces
    across_flux = across * (padded[..., 1:] - padded[..., :-1])
    leakage = leakage - across_flux[..., 1:] + across_flux[..., :-1]
    spread = spread + across[..., 1:] + across[..., :-1]
    return (leakage, spread)


def coefficients(temper, droplet):
    heat = jnp.broadcast_to(cond_oil + (cond_drop - cond_oil) * droplet, temper.shape)
    ions = (diff_oil + (diff_drop - diff_oil) * droplet) * jnp.exp(thermal_slope * temper)
    return jnp.stack([heat, ions], axis=0)


def face_mask(offset, total, margin, columns):
    place = offset - margin + jnp.arange(columns + 2 * margin - 1, dtype=jnp.int32)
    return ((place >= 0) & (place + 1 <= total - 1)).astype(jnp.float32)


def column_rims(values):
    return padded_2(values, (("gy", 3),), 1)


def shards(fields, phase, electrode, planes):
    state = fields.astype(jnp.float32)
    height = state.shape[1]
    width_x = state.shape[2]
    columns = state.shape[3]
    steps = electrode.shape[0]
    static = jnp.concatenate([phase[None], electrode], axis=0)
    static_width = 2
    static_pad = padded_2(static, (("gy", 2),), static_width)
    offset = lax.axis_index("gy") * columns
    total = columns * lax.axis_size("gy")
    depth_decay = jnp.exp(-4.0 * jnp.arange(height, dtype=jnp.float32) / height)[:, None, None]
    plane_index = jnp.arange(width_x, dtype=jnp.int32)[:, None]
    is_first = (plane_index == 0).astype(jnp.float32)
    is_last = (plane_index == width_x - 1).astype(jnp.float32)
    edge = is_first + is_last
    rims = padded_2(planes, (("gx", 3),), 2)
    left_all = rims[:, :, :, 1] + extrap_half * (rims[:, :, :, 1] - rims[:, :, :, 0])
    right_all = rims[:, :, :, 6] + extrap_half * (rims[:, :, :, 6] - rims[:, :, :, 7])
    droplet_all = static_pad[0].astype(jnp.float32)
    faces_one = face_mask(offset, total, 1, columns)
    outputs = []
    for step in range(steps):
        active_all = static_pad[1 + step].astype(jnp.float32)
        left_step = left_all[step]
        right_step = right_all[step]
        padded = column_rims(state)
        droplet_k = droplet_all[:, 1:-1]
        droplet_q = droplet_all[:, 2:-2]
        active_q = active_all[:, 2:-2]
        conduct = coefficients(padded[0], droplet_k)
        centre = padded[..., 1:-1]
        robin = robin_weight * conduct[..., 1:-1] * edge
        leakage, spread = couple(padded, conduct, faces_one)
        diagonal = 1.0 + time_step * (spread + robin)
        heat_src = (
            joule_rate * active_q * droplet_q * (1.0 + 0.5 * centre[1] * centre[1]) * depth_decay
        )
        source = jnp.stack([heat_src, jnp.zeros_like(heat_src)], axis=0)
        trace = left_step[:, :, None, :] * is_first + right_step[:, :, None, :] * is_last
        target = centre + time_step * (source + robin * trace)
        residual = target - (centre + time_step * (leakage + robin * centre))
        move = residual / diagonal / cheb_centre
        first = centre + move
        first_pad = column_rims(first)
        leak_first, spread_unused = couple(first_pad, conduct, faces_one)
        residual_first = target - (first + time_step * (leak_first + robin * first))
        state = (
            first
            + rho_second * rho_first * move
            + 2.0 * rho_second / cheb_radius * residual_first / diagonal
        )
        outputs.append(
            jnp.stack([state[:, :, 0], state[:, :, 1], state[:, :, -2], state[:, :, -1]], axis=2)
        )
    return (state, jnp.stack(outputs, axis=0))


def solution(mesh):
    placed = (
        P(None, None, "gx", "gy"),
        P("gx", "gy"),
        P(None, "gx", "gy"),
        P(None, None, None, "gx", "gy"),
    )
    return jax.shard_map(
        shards,
        mesh=mesh,
        in_specs=placed,
        out_specs=(P(None, None, "gx", "gy"), P(None, None, None, "gx", "gy")),
        check_vma=False,
    )
```

profile of v0, /device:TPU:24, one launch (start us, length us, event | category | flops | bytes accessed | tf_op | source)
XLA Modules:
  0.0 73.8 jit_solution(3486392749533646610)
XLA Ops:
  0.7 1.1 %fusion.121 = (f32[2,16,16,1]{3,2,1,0:T(8,128)S(1)}, f32[2,16,16,1]{3,2,1,0:T(8,128)S(1)}) fusion(bf16[2,16,16,128]{3,2,1,0:T(8,128)(2,1)} %param.4), kind=kLoop, calls=%fused_computation.181 | loop fusion | bytes 8192 | tf_op jit(solution)/shard_map/slice | solution.py:27
  1.8 4.8 %collective-permute-start.3 = (f32[2,16,16,1]{3,2,1,0:T(8,128)S(1)}, f32[2,16,16,1]{3,2,1,0:T(8,128)S(1)}, u32[]{:S(2)}, u32[]{:S(2)}) collective-permute-start(f32[2,16,16,1]{3,2,1,0:T(8,128)S(1)} %get-tuple-element.45), channel_id=1, source_target_pairs={{1,0},{2,1},{3,2},{4,3},{5,4},{6,5},{7,6},{8,7},{9,8},{10,9},{11,1... | collective-permute-start | bytes 6152 | tf_op jit(solution)/shard_map/ppermute | solution.py:32
  6.6 1.9 %collective-permute-start.2 = (f32[2,16,16,1]{3,2,1,0:T(8,128)S(1)}, f32[2,16,16,1]{3,2,1,0:T(8,128)S(1)}, u32[]{:S(2)}, u32[]{:S(2)}) collective-permute-start(f32[2,16,16,1]{3,2,1,0:T(8,128)S(1)} %get-tuple-element.44), channel_id=1, source_target_pairs={{0,1},{1,2},{2,3},{3,4},{4,5},{5,6},{6,7},{7,8},{8,9},{9,10},{10,1... | collective-permute-start | bytes 6152 | tf_op jit(solution)/shard_map/ppermute | solution.py:30
  8.6 6.0 %collective-permute-start.1 = (s32[3,16,2]{2,1,0:T(8,128)S(1)}, s32[3,16,2]{2,1,0:T(8,128)S(1)}, u32[]{:S(2)}, u32[]{:S(2)}) collective-permute-start(s32[3,16,2]{2,1,0:T(8,128)S(1)} %get-tuple-element.56), channel_id=1, source_target_pairs={{1,0},{2,1},{3,2},{4,3},{5,4},{6,5},{7,6},{8,7},{9,8},{10,9},{11,1... | collective-permute-start | bytes 1160 | tf_op jit(solution)/shard_map/ppermute | solution.py:32
  14.7 2.1 %collective-permute-start = (s32[3,16,2]{2,1,0:T(8,128)S(1)}, s32[3,16,2]{2,1,0:T(8,128)S(1)}, u32[]{:S(2)}, u32[]{:S(2)}) collective-permute-start(s32[3,16,2]{2,1,0:T(8,128)S(1)} %get-tuple-element.55), channel_id=1, source_target_pairs={{0,1},{1,2},{2,3},{3,4},{4,5},{5,6},{6,7},{7,8},{8,9},{9,10},{10,1... | collective-permute-start | bytes 1160 | tf_op jit(solution)/shard_map/ppermute | solution.py:30
  16.8 1.3 %collective-permute-start.5 = (f32[2,2,16,2,128]{4,3,2,1,0:T(2,128)S(1)}, f32[2,2,16,2,128]{4,3,2,1,0:T(2,128)S(1)}, u32[]{:S(2)}, u32[]{:S(2)}) collective-permute-start(f32[2,2,16,2,128]{4,3,2,1,0:T(2,128)S(1)} %get-tuple-element.43), channel_id=1, source_target_pairs={{16,0},{32,16},{48,32},{64,48},{80,64},{96,80},{112,96},{17,1},{33... | collective-permute-start | bytes 196616 | tf_op jit(solution)/shard_map/ppermute | solution.py:32
  18.2 3.0 %collective-permute-start.4 = (f32[2,2,16,2,128]{4,2,1,0,3:T(8,128)S(1)}, f32[2,2,16,2,128]{4,2,1,0,3:T(8,128)S(1)}, u32[]{:S(2)}, u32[]{:S(2)}) collective-permute-start(f32[2,2,16,2,128]{4,2,1,0,3:T(8,128)S(1)} %copy.8), channel_id=1, source_target_pairs={{0,16},{16,32},{32,48},{48,64},{64,80},{80,96},{96,112},{1,17},{17... | collective-permute-start | bytes 196616 | tf_op jit(solution)/shard_map/ppermute | solution.py:30
  21.3 1.4 %collective-permute-done = s32[3,16,2]{2,1,0:T(8,128)S(1)} collective-permute-done((s32[3,16,2]{2,1,0:T(8,128)S(1)}, s32[3,16,2]{2,1,0:T(8,128)S(1)}, u32[]{:S(2)}, u32[]{:S(2)}) %collective-permute-start) | collective-permute-done | bytes 416 | tf_op jit(solution)/shard_map/ppermute | solution.py:30
  24.2 0.4 convert_add_fusion
  24.8 4.7 %collective-permute-start.6 = (f32[2,16,16,1]{3,2,1,0:T(8,128)S(1)}, f32[2,16,16,1]{3,2,1,0:T(8,128)S(1)}, u32[]{:S(2)}, u32[]{:S(2)}) collective-permute-start(f32[2,16,16,1]{3,2,1,0:T(8,128)S(1)} %get-tuple-element.41), channel_id=1, source_target_pairs={{1,0},{2,1},{3,2},{4,3},{5,4},{6,5},{7,6},{8,7},{9,8},{10,9},{11,1... | collective-permute-start | bytes 6152 | tf_op jit(solution)/shard_map/ppermute | solution.py:32
  29.5 1.9 %collective-permute-start.7 = (f32[2,16,16,1]{3,2,1,0:T(8,128)S(1)}, f32[2,16,16,1]{3,2,1,0:T(8,128)S(1)}, u32[]{:S(2)}, u32[]{:S(2)}) collective-permute-start(f32[2,16,16,1]{3,2,1,0:T(8,128)S(1)} %get-tuple-element.40), channel_id=1, source_target_pairs={{0,1},{1,2},{2,3},{3,4},{4,5},{5,6},{6,7},{7,8},{8,9},{9,10},{10,1... | collective-permute-start | bytes 6152 | tf_op jit(solution)/shard_map/ppermute | solution.py:30
  31.4 4.2 %collective-permute-done.6 = f32[2,16,16,1]{3,2,1,0:T(8,128)S(1)} collective-permute-done((f32[2,16,16,1]{3,2,1,0:T(8,128)S(1)}, f32[2,16,16,1]{3,2,1,0:T(8,128)S(1)}, u32[]{:S(2)}, u32[]{:S(2)}) %collective-permute-start.6) | collective-permute-done | bytes 2080 | tf_op jit(solution)/shard_map/ppermute | solution.py:32
  35.6 6.7 %collective-permute-done.7 = f32[2,16,16,1]{3,2,1,0:T(8,128)S(1)} collective-permute-done((f32[2,16,16,1]{3,2,1,0:T(8,128)S(1)}, f32[2,16,16,1]{3,2,1,0:T(8,128)S(1)}, u32[]{:S(2)}, u32[]{:S(2)}) %collective-permute-start.7) | collective-permute-done | bytes 2080 | tf_op jit(solution)/shard_map/ppermute | solution.py:30
  42.6 0.4 fusion.52
  43.1 1.9 %collective-permute-start.9 = (f32[2,16,16,1]{3,2,1,0:T(8,128)S(1)}, f32[2,16,16,1]{3,2,1,0:T(8,128)S(1)}, u32[]{:S(2)}, u32[]{:S(2)}) collective-permute-start(f32[2,16,16,1]{3,2,1,0:T(8,128)S(1)} %get-tuple-element.39), channel_id=1, source_target_pairs={{1,0},{2,1},{3,2},{4,3},{5,4},{6,5},{7,6},{8,7},{9,8},{10,9},{11,1... | collective-permute-start | bytes 6152 | tf_op jit(solution)/shard_map/ppermute | solution.py:32
  45.1 3.9 %collective-permute-start.8 = (f32[2,16,16,1]{3,2,1,0:T(8,128)S(1)}, f32[2,16,16,1]{3,2,1,0:T(8,128)S(1)}, u32[]{:S(2)}, u32[]{:S(2)}) collective-permute-start(f32[2,16,16,1]{3,2,1,0:T(8,128)S(1)} %get-tuple-element.38), channel_id=1, source_target_pairs={{0,1},{1,2},{2,3},{3,4},{4,5},{5,6},{6,7},{7,8},{8,9},{9,10},{10,1... | collective-permute-start | bytes 6152 | tf_op jit(solution)/shard_map/ppermute | solution.py:30
  49.1 4.2 %collective-permute-done.9 = f32[2,16,16,1]{3,2,1,0:T(8,128)S(1)} collective-permute-done((f32[2,16,16,1]{3,2,1,0:T(8,128)S(1)}, f32[2,16,16,1]{3,2,1,0:T(8,128)S(1)}, u32[]{:S(2)}, u32[]{:S(2)}) %collective-permute-start.9) | collective-permute-done | bytes 2080 | tf_op jit(solution)/shard_map/ppermute | solution.py:32
  53.4 4.0 %collective-permute-done.8 = f32[2,16,16,1]{3,2,1,0:T(8,128)S(1)} collective-permute-done((f32[2,16,16,1]{3,2,1,0:T(8,128)S(1)}, f32[2,16,16,1]{3,2,1,0:T(8,128)S(1)}, u32[]{:S(2)}, u32[]{:S(2)}) %collective-permute-start.8) | collective-permute-done | bytes 2080 | tf_op jit(solution)/shard_map/ppermute | solution.py:30
  58.4 0.4 fusion.92
  59.0 1.9 %collective-permute-start.10 = (f32[2,16,16,1]{3,2,1,0:T(8,128)S(1)}, f32[2,16,16,1]{3,2,1,0:T(8,128)S(1)}, u32[]{:S(2)}, u32[]{:S(2)}) collective-permute-start(f32[2,16,16,1]{3,2,1,0:T(8,128)S(1)} %get-tuple-element.37), channel_id=1, source_target_pairs={{1,0},{2,1},{3,2},{4,3},{5,4},{6,5},{7,6},{8,7},{9,8},{10,9},{11,1... | collective-permute-start | bytes 6152 | tf_op jit(solution)/shard_map/ppermute | solution.py:32
  60.9 3.9 %collective-permute-start.11 = (f32[2,16,16,1]{3,2,1,0:T(8,128)S(1)}, f32[2,16,16,1]{3,2,1,0:T(8,128)S(1)}, u32[]{:S(2)}, u32[]{:S(2)}) collective-permute-start(f32[2,16,16,1]{3,2,1,0:T(8,128)S(1)} %get-tuple-element.36), channel_id=1, source_target_pairs={{0,1},{1,2},{2,3},{3,4},{4,5},{5,6},{6,7},{7,8},{8,9},{9,10},{10,1... | collective-permute-start | bytes 6152 | tf_op jit(solution)/shard_map/ppermute | solution.py:30
  64.9 3.5 %collective-permute-done.10 = f32[2,16,16,1]{3,2,1,0:T(8,128)S(1)} collective-permute-done((f32[2,16,16,1]{3,2,1,0:T(8,128)S(1)}, f32[2,16,16,1]{3,2,1,0:T(8,128)S(1)}, u32[]{:S(2)}, u32[]{:S(2)}) %collective-permute-start.10) | collective-permute-done | bytes 2080 | tf_op jit(solution)/shard_map/ppermute | solution.py:32
  68.4 4.0 %collective-permute-done.11 = f32[2,16,16,1]{3,2,1,0:T(8,128)S(1)} collective-permute-done((f32[2,16,16,1]{3,2,1,0:T(8,128)S(1)}, f32[2,16,16,1]{3,2,1,0:T(8,128)S(1)}, u32[]{:S(2)}, u32[]{:S(2)}) %collective-permute-start.11) | collective-permute-done | bytes 2080 | tf_op jit(solution)/shard_map/ppermute | solution.py:30
  73.1 0.7 pad_maximum_fusion.6
  (57 shorter events, 4.1 us)
Async XLA Ops:
  0.6 7.9 %copy-start.3 = (s32[2,16,128]{2,1,0:T(8,128)S(1)}, s32[2,16,128]{2,1,0:T(8,128)}, u32[]{:S(2)}) copy-start(s32[2,16,128]{2,1,0:T(8,128)} %param.6) | copy-start | bytes 49156
  0.6 7.9 %copy-start.4 = (s32[16,128]{1,0:T(8,128)S(1)}, s32[16,128]{1,0:T(8,128)}, u32[]{:S(2)}) copy-start(s32[16,128]{1,0:T(8,128)} %param.5) | copy-start | bytes 24580
  0.7 16.1 %copy-start.2 = (f32[2,2,16,4,128]{4,3,2,1,0:T(4,128)S(1)}, f32[2,2,16,4,128]{4,3,2,1,0:T(4,128)}, u32[]{:S(2)}) copy-start(f32[2,2,16,4,128]{4,3,2,1,0:T(4,128)} %param.7) | copy-start | bytes 393220
  1.8 21.2 %collective-permute-start.3 = (f32[2,16,16,1]{3,2,1,0:T(8,128)S(1)}, f32[2,16,16,1]{3,2,1,0:T(8,128)S(1)}, u32[]{:S(2)}, u32[]{:S(2)}) collective-permute-start(f32[2,16,16,1]{3,2,1,0:T(8,128)S(1)} %get-tuple-element.45), channel_id=1, source_target_pairs={{1,0},{2,1},{3,2},{4,3},{5,4},{6,5},{7,6},{8,7},{9,8},{10,9},{11,1... | collective-permute-start | bytes 6152 | tf_op jit(solution)/shard_map/ppermute | solution.py:32
  6.6 16.4 %collective-permute-start.2 = (f32[2,16,16,1]{3,2,1,0:T(8,128)S(1)}, f32[2,16,16,1]{3,2,1,0:T(8,128)S(1)}, u32[]{:S(2)}, u32[]{:S(2)}) collective-permute-start(f32[2,16,16,1]{3,2,1,0:T(8,128)S(1)} %get-tuple-element.44), channel_id=1, source_target_pairs={{0,1},{1,2},{2,3},{3,4},{4,5},{5,6},{6,7},{7,8},{8,9},{9,10},{10,1... | collective-permute-start | bytes 6152 | tf_op jit(solution)/shard_map/ppermute | solution.py:30
  8.6 9.6 %collective-permute-start.1 = (s32[3,16,2]{2,1,0:T(8,128)S(1)}, s32[3,16,2]{2,1,0:T(8,128)S(1)}, u32[]{:S(2)}, u32[]{:S(2)}) collective-permute-start(s32[3,16,2]{2,1,0:T(8,128)S(1)} %get-tuple-element.56), channel_id=1, source_target_pairs={{1,0},{2,1},{3,2},{4,3},{5,4},{6,5},{7,6},{8,7},{9,8},{10,9},{11,1... | collective-permute-start | bytes 1160 | tf_op jit(solution)/shard_map/ppermute | solution.py:32
  14.7 3.5 %copy-start = (bf16[2,16,16,128]{3,2,1,0:T(8,128)(2,1)S(1)}, bf16[2,16,16,128]{3,2,1,0:T(8,128)(2,1)}, u32[]{:S(2)}) copy-start(bf16[2,16,16,128]{3,2,1,0:T(8,128)(2,1)} %param.4) | copy-start | bytes 393220
  14.7 8.0 %collective-permute-start = (s32[3,16,2]{2,1,0:T(8,128)S(1)}, s32[3,16,2]{2,1,0:T(8,128)S(1)}, u32[]{:S(2)}, u32[]{:S(2)}) collective-permute-start(s32[3,16,2]{2,1,0:T(8,128)S(1)} %get-tuple-element.55), channel_id=1, source_target_pairs={{0,1},{1,2},{2,3},{3,4},{4,5},{5,6},{6,7},{7,8},{8,9},{9,10},{10,1... | collective-permute-start | bytes 1160 | tf_op jit(solution)/shard_map/ppermute | solution.py:30
  16.8 7.2 %collective-permute-start.5 = (f32[2,2,16,2,128]{4,3,2,1,0:T(2,128)S(1)}, f32[2,2,16,2,128]{4,3,2,1,0:T(2,128)S(1)}, u32[]{:S(2)}, u32[]{:S(2)}) collective-permute-start(f32[2,2,16,2,128]{4,3,2,1,0:T(2,128)S(1)} %get-tuple-element.43), channel_id=1, source_target_pairs={{16,0},{32,16},{48,32},{64,48},{80,64},{96,80},{112,96},{17,1},{33... | collective-permute-start | bytes 196616 | tf_op jit(solution)/shard_map/ppermute | solution.py:32
  18.2 5.9 %collective-permute-start.4 = (f32[2,2,16,2,128]{4,2,1,0,3:T(8,128)S(1)}, f32[2,2,16,2,128]{4,2,1,0,3:T(8,128)S(1)}, u32[]{:S(2)}, u32[]{:S(2)}) collective-permute-start(f32[2,2,16,2,128]{4,2,1,0,3:T(8,128)S(1)} %copy.8), channel_id=1, source_target_pairs={{0,16},{16,32},{32,48},{48,64},{64,80},{80,96},{96,112},{1,17},{17... | collective-permute-start | bytes 196616 | tf_op jit(solution)/shard_map/ppermute | solution.py:30
  24.8 10.8 %collective-permute-start.6 = (f32[2,16,16,1]{3,2,1,0:T(8,128)S(1)}, f32[2,16,16,1]{3,2,1,0:T(8,128)S(1)}, u32[]{:S(2)}, u32[]{:S(2)}) collective-permute-start(f32[2,16,16,1]{3,2,1,0:T(8,128)S(1)} %get-tuple-element.41), channel_id=1, source_target_pairs={{1,0},{2,1},{3,2},{4,3},{5,4},{6,5},{7,6},{8,7},{9,8},{10,9},{11,1... | collective-permute-start | bytes 6152 | tf_op jit(solution)/shard_map/ppermute | solution.py:32
  29.5 12.9 %collective-permute-start.7 = (f32[2,16,16,1]{3,2,1,0:T(8,128)S(1)}, f32[2,16,16,1]{3,2,1,0:T(8,128)S(1)}, u32[]{:S(2)}, u32[]{:S(2)}) collective-permute-start(f32[2,16,16,1]{3,2,1,0:T(8,128)S(1)} %get-tuple-element.40), channel_id=1, source_target_pairs={{0,1},{1,2},{2,3},{3,4},{4,5},{5,6},{6,7},{7,8},{8,9},{9,10},{10,1... | collective-permute-start | bytes 6152 | tf_op jit(solution)/shard_map/ppermute | solution.py:30
  43.1 10.2 %collective-permute-start.9 = (f32[2,16,16,1]{3,2,1,0:T(8,128)S(1)}, f32[2,16,16,1]{3,2,1,0:T(8,128)S(1)}, u32[]{:S(2)}, u32[]{:S(2)}) collective-permute-start(f32[2,16,16,1]{3,2,1,0:T(8,128)S(1)} %get-tuple-element.39), channel_id=1, source_target_pairs={{1,0},{2,1},{3,2},{4,3},{5,4},{6,5},{7,6},{8,7},{9,8},{10,9},{11,1... | collective-permute-start | bytes 6152 | tf_op jit(solution)/shard_map/ppermute | solution.py:32
  45.1 12.3 %collective-permute-start.8 = (f32[2,16,16,1]{3,2,1,0:T(8,128)S(1)}, f32[2,16,16,1]{3,2,1,0:T(8,128)S(1)}, u32[]{:S(2)}, u32[]{:S(2)}) collective-permute-start(f32[2,16,16,1]{3,2,1,0:T(8,128)S(1)} %get-tuple-element.38), channel_id=1, source_target_pairs={{0,1},{1,2},{2,3},{3,4},{4,5},{5,6},{6,7},{7,8},{8,9},{9,10},{10,1... | collective-permute-start | bytes 6152 | tf_op jit(solution)/shard_map/ppermute | solution.py:30
  59.0 9.4 %collective-permute-start.10 = (f32[2,16,16,1]{3,2,1,0:T(8,128)S(1)}, f32[2,16,16,1]{3,2,1,0:T(8,128)S(1)}, u32[]{:S(2)}, u32[]{:S(2)}) collective-permute-start(f32[2,16,16,1]{3,2,1,0:T(8,128)S(1)} %get-tuple-element.37), channel_id=1, source_target_pairs={{1,0},{2,1},{3,2},{4,3},{5,4},{6,5},{7,6},{8,7},{9,8},{10,9},{11,1... | collective-permute-start | bytes 6152 | tf_op jit(solution)/shard_map/ppermute | solution.py:32
  60.9 11.5 %collective-permute-start.11 = (f32[2,16,16,1]{3,2,1,0:T(8,128)S(1)}, f32[2,16,16,1]{3,2,1,0:T(8,128)S(1)}, u32[]{:S(2)}, u32[]{:S(2)}) collective-permute-start(f32[2,16,16,1]{3,2,1,0:T(8,128)S(1)} %get-tuple-element.36), channel_id=1, source_target_pairs={{0,1},{1,2},{2,3},{3,4},{4,5},{5,6},{6,7},{7,8},{8,9},{9,10},{10,1... | collective-permute-start | bytes 6152 | tf_op jit(solution)/shard_map/ppermute | solution.py:30
  73.0 0.8 %copy-start.1 = (f32[2,16,16,128]{3,2,1,0:T(8,128)}, f32[2,16,16,128]{3,2,1,0:T(8,128)S(1)}, u32[]{:S(2)}) copy-start(f32[2,16,16,128]{3,2,1,0:T(8,128)S(1)} %fusion.32) | copy-start | bytes 786436
where the time goes:
time: 74.2 us; the launch traced here: 73.8 us
  starting transfers between devices  37.4 us (50%)
  waiting for transfers between devices  28.1 us (38%)
  other arithmetic  5.4 us (7%)
  local copies, waits for them, and re-layouts  1.72 us (2%)
  between operations  1.1 us (1%)
    ppermute x6, starting transfers between devices, padded_2(): lax.ppermute(head, axis, [((i + 1) % count, i) for i in range(ends)])  20.7 us
    ppermute x6, starting transfers between devices, padded_2(): lax.ppermute(tail, axis, [(i, (i + 1) % count) for i in range(ends)])  16.8 us
    ppermute x6, waiting for transfers between devices, padded_2(): lax.ppermute(tail, axis, [(i, (i + 1) % count) for i in range(ends)])  16.2 us
    ppermute x6, waiting for transfers between devices, padded_2(): lax.ppermute(head, axis, [((i + 1) % count, i) for i in range(ends)])  11.9 us
    slice x5, local copies, waits for them, and re-layouts, padded_2(): lax.slice_in_dim(cells, cells.shape[dim] - width, cells.shape[dim], axis=...  1.55 us
  transfers between devices with their start and end apart: 12, of which 7 were waited for; matrix products, arithmetic and copies ran while one was open for 2% of the time, Pallas kernels for 0%

commit v1 on v0

v1 whole, which is shorter than its diff:
```python
import functools

import jax
import jax.numpy as jnp
from jax import lax
from jax.experimental import pallas as pl
from jax.experimental.pallas import tpu as pltpu
from jax.sharding import PartitionSpec as P

MESH = pl.DeviceIdType.MESH
cond_oil = 0.6
cond_drop = 2.0
diff_oil = 0.3
diff_drop = 1.0
thermal_slope = 0.3
cheb_radius = 0.95
cheb_ratio = 1.0 / cheb_radius
rho_first = 1.0 / cheb_ratio
rho_second = 1.0 / (2.0 * cheb_ratio - rho_first)
keep_old = rho_second * rho_first
take_new = 2.0 * rho_second / cheb_radius

Z = 16
X = 16
C = 128
CORNERS = ((-1, -1), (-1, 1), (1, -1), (1, 1))
SIDES_Y = ((0, -1), (0, 1))
SIDES_X = ((-1, 0), (1, 0))
ALL = CORNERS + SIDES_Y + SIDES_X


def lanes(shape):
    return lax.broadcasted_iota(jnp.int32, shape, len(shape) - 1)


def roll_last(v, shift):
    return pltpu.roll(v, shift % C, v.ndim - 1)


def roll_rows(v, shift):
    return pltpu.roll(v, shift % X, v.ndim - 2)


def row_masks(ndim):
    shape = (1,) * (ndim - 2) + (X, C)
    rows = lax.broadcasted_iota(jnp.int32, shape, ndim - 2)
    return rows


def packed_columns(v):
    head = v.shape[:-3]
    v = v.reshape(head + (2, 8, X, C))
    lane = lanes(head + (2, X, C))
    out = None
    for j in range(8):
        moved = roll_last(v[..., j, :, :], 16 * j + 8)
        out = moved if out is None else jnp.where(lane >= 16 * j, moved, out)
    return out


def packed_map(v):
    base = jnp.where(lanes(v.shape) < 16, roll_last(v, 8), 0.0)
    base = base + roll_last(base, 16)
    base = base + roll_last(base, 32)
    return base + roll_last(base, 64)


def steps_of(droplet, active, old_t, old_n, trace, decay, shifts, masks):
    xp, xm, yp, ym, zp, zm = shifts
    mxp, mxm, myp, mym, mzp, mzm, edge4 = masks

    def coefficients(k):
        faces = (
            (k + xp(k)) * mxp,
            (k + xm(k)) * mxm,
            (k + yp(k)) * myp,
            (k + ym(k)) * mym,
            (k + zp(k)) * mzp,
            (k + zm(k)) * mzm,
        )
        robin = k * edge4
        diagonal = 1.0 + robin + sum(faces[1:], faces[0])
        return faces, robin, 1.0 / diagonal

    def sweep(v, target, faces):
        total = target
        for face, move in zip(faces, shifts):
            total = total + face * move(v)
        return total

    heat = jnp.broadcast_to(cond_oil + (cond_drop - cond_oil) * droplet, old_t.shape)
    ion_base = diff_oil + (diff_drop - diff_oil) * droplet
    heat_faces, heat_robin, heat_inv = coefficients(heat)
    states = []
    for step in range(2):
        ions = ion_base * jnp.exp(thermal_slope * old_t)
        source = (active[step] * droplet) * decay * (1.0 + 0.5 * old_n * old_n)
        target_t = old_t + source + heat_robin * trace(step, 0)
        first = sweep(old_t, target_t, heat_faces) * heat_inv
        new_t = sweep(first, target_t, heat_faces) * (take_new * heat_inv) - keep_old * old_t
        ion_faces, ion_robin, ion_inv = coefficients(ions)
        target_n = old_n + ion_robin * trace(step, 1)
        first = sweep(old_n, target_n, ion_faces) * ion_inv
        new_n = sweep(first, target_n, ion_faces) * (take_new * ion_inv) - keep_old * old_n
        old_t, old_n = new_t, new_n
        states.append((old_t, old_n))
    return states


def kernel(
    n_gx,
    n_gy,
    f_hbm,
    ph_hbm,
    el_hbm,
    pl_hbm,
    of_ref,
    op_ref,
    f_in,
    ph_in,
    el_in,
    pl_in,
    send_b,
    send_g,
    recv_b,
    recv_g,
    recv_c,
    in_sem,
    send_sem,
    recv_sem,
):
    gx = lax.axis_index("gx")
    gy = lax.axis_index("gy")

    def exists(offset):
        found = []
        for place, move, count in ((gx, offset[0], n_gx), (gy, offset[1], n_gy)):
            if move < 0:
                found.append(place > 0)
            if move > 0:
                found.append(place < count - 1)
        return functools.reduce(jnp.logical_and, found)

    def at(offset):
        return (gx + offset[0], gy + offset[1])

    barrier = pltpu.get_barrier_semaphore()
    expected = jnp.int32(0)
    for offset in ALL:

        @pl.when(exists(offset))
        def _(offset=offset):
            pl.semaphore_signal(barrier, inc=1, device_id=at(offset), device_id_type=MESH)

        expected = expected + exists(offset).astype(jnp.int32)

    loads = [
        pltpu.make_async_copy(src, dst, in_sem.at[i])
        for i, (src, dst) in enumerate(((ph_hbm, ph_in), (el_hbm, el_in), (f_hbm, f_in), (pl_hbm, pl_in)))
    ]
    for load in loads:
        load.start()

    for i, offset in enumerate(SIDES_Y):

        @pl.when(jnp.logical_not(exists(offset)))
        def _(i=i):
            recv_b[i] = jnp.zeros(recv_b.shape[1:], jnp.float32)

    for i, offset in enumerate(SIDES_X):

        @pl.when(jnp.logical_not(exists(offset)))
        def _(i=i):
            recv_g[i] = jnp.zeros(recv_g.shape[1:], jnp.float32)

    for i, offset in enumerate(CORNERS):

        @pl.when(jnp.logical_not(exists(offset)))
        def _(i=i):
            recv_c[i] = jnp.zeros(recv_c.shape[1:], jnp.float32)

    loads[0].wait()
    loads[1].wait()
    send_b[4] = packed_map(ph_in[...].astype(jnp.float32))
    send_b[5] = packed_map(el_in[0].astype(jnp.float32))
    send_b[6] = packed_map(el_in[1].astype(jnp.float32))
    loads[2].wait()
    send_b[0:4] = packed_columns(f_in[...].astype(jnp.float32)).reshape(4, X, C)
    loads[3].wait()
    own_row = lax.broadcasted_iota(jnp.int32, (Z, C), 0) % 8 == lanes((Z, C)) // 16
    for side in range(2):
        near, far = ((0, 1), (3, 2))[side]
        for s in range(2):
            for f in range(2):
                a = pl_in[s, f, :, near, :]
                b = pl_in[s, f, :, far, :]
                g = a + 0.5 * (a - b)
                row = (s * 2 + f) * Z
                send_g[side, row : row + Z, :] = g
                spread = pltpu.roll(g, 8, 1, stride=16, stride_axis=0)
                spread = jnp.where(own_row, spread, 0.0).reshape(2, 8, C)
                row = 64 + (s * 2 + f) * 2
                send_g[side, row : row + 2, :] = jnp.sum(spread, axis=1)

    pl.semaphore_wait(barrier, expected)

    def copy_of(i, offset):
        back = (-offset[0], -offset[1])
        if offset in CORNERS:
            src = send_g.at[(offset[0] + 1) // 2, pl.ds(64, 8)]
            dst = recv_c.at[CORNERS.index(back)]
        elif offset in SIDES_Y:
            src = send_b
            dst = recv_b.at[SIDES_Y.index(back)]
        else:
            src = send_g.at[(offset[0] + 1) // 2]
            dst = recv_g.at[SIDES_X.index(back)]
        return pltpu.make_async_remote_copy(
            src_ref=src,
            dst_ref=dst,
            send_sem=send_sem.at[i],
            recv_sem=recv_sem.at[ALL.index(back)],
            device_id=at(offset),
            device_id_type=MESH,
        )

    for i, offset in enumerate(ALL):

        @pl.when(exists(offset))
        def _(i=i, offset=offset):
            copy_of(i, offset).start()

    def wait_from(offset):
        back = (-offset[0], -offset[1])

        @pl.when(exists(offset))
        def _():
            copy_of(ALL.index(back), back).wait_recv()

    for offset in SIDES_X:
        wait_from(offset)

    rows = row_masks(3)
    layer = lax.broadcasted_iota(jnp.int32, (Z, 1, 1), 0)
    one = jnp.float32(1.0)
    masks = (
        (rows < X - 1).astype(jnp.float32),
        (rows > 0).astype(jnp.float32),
        one,
        one,
        (layer < Z - 1).astype(jnp.float32),
        (layer > 0).astype(jnp.float32),
        jnp.where((rows == 0) | (rows == X - 1), 4.0, 0.0),
    )
    shifts = (
        lambda v: roll_rows(v, -1),
        lambda v: roll_rows(v, 1),
        lambda v: roll_last(v, -1),
        lambda v: roll_last(v, 1),
        lambda v: jnp.concatenate([v[1:], v[:1]], axis=0),
        lambda v: jnp.concatenate([v[-1:], v[:-1]], axis=0),
    )

    def trace_own(step, field):
        row = (step * 2 + field) * Z
        lo = jnp.broadcast_to(recv_g[0, row : row + Z, :][:, None, :], (Z, 8, C))
        hi = jnp.broadcast_to(recv_g[1, row : row + Z, :][:, None, :], (Z, 8, C))
        return jnp.concatenate([lo, hi], axis=1)

    decay = jnp.exp(-4.0 * layer.astype(jnp.float32) / Z)
    active = [el_in[s].astype(jnp.float32)[None] for s in range(2)]
    states = steps_of(
        ph_in[...].astype(jnp.float32)[None],
        active,
        f_in[0].astype(jnp.float32),
        f_in[1].astype(jnp.float32),
        trace_own,
        decay,
        shifts,
        masks,
    )
    for f in range(2):
        op_ref[0, f, :, 0:2, :] = states[0][f][:, 0:2, :]
        op_ref[0, f, :, 2:4, :] = states[0][f][:, 14:16, :]
        of_ref[f] = states[1][f]

    for offset in SIDES_Y + CORNERS:
        wait_from(offset)

    lane = lanes((1, 1, 1, C))
    column = lane % 16
    inner = column < 8
    rows = row_masks(4)
    half = lax.broadcasted_iota(jnp.int32, (1, 2, 1, 1), 1)
    layer = half * 8 + lane // 16
    left_open = (gy > 0).astype(jnp.float32)
    right_open = (gy < n_gy - 1).astype(jnp.float32)
    side = lax.broadcasted_iota(jnp.int32, (2, 1, 1, 1), 0)
    opened = jnp.where(side == 0, left_open, right_open)
    masks = (
        (rows < X - 1).astype(jnp.float32),
        (rows > 0).astype(jnp.float32),
        jnp.where(column == 7, opened, 1.0),
        jnp.where(column == 8, opened, 1.0),
        (layer < Z - 1).astype(jnp.float32),
        (layer > 0).astype(jnp.float32),
        jnp.where((rows == 0) | (rows == X - 1), 4.0, 0.0),
    )

    def swap(v):
        return jnp.concatenate([v[:, 1:2], v[:, 0:1]], axis=1)

    def layer_up(v):
        moved = roll_last(v, -16)
        return jnp.where(lane < 112, moved, swap(moved))

    def layer_down(v):
        moved = roll_last(v, 16)
        return jnp.where(lane >= 16, moved, swap(moved))

    shifts = (
        lambda v: roll_rows(v, -1),
        lambda v: roll_rows(v, 1),
        lambda v: roll_last(v, -1),
        lambda v: roll_last(v, 1),
        layer_up,
        layer_down,
    )

    def strip(first, last):
        own = send_b[first:last]
        inside = inner[0]
        return jnp.stack(
            [jnp.where(inside, recv_b[0, first:last], own), jnp.where(inside, own, recv_b[1, first:last])], axis=0
        )

    def trace_strip(step, field):
        row = (step * 2 + field) * 2
        halves = []
        for i in range(2):
            mid = recv_g[i, 64 + row : 66 + row, :]
            low = jnp.where(inner[0, 0], recv_c[2 * i, row : row + 2, :], mid)
            high = jnp.where(inner[0, 0], mid, recv_c[2 * i + 1, row : row + 2, :])
            both = jnp.stack([low, high], axis=0)[:, :, None, :]
            halves.append(jnp.broadcast_to(both, (2, 2, 8, C)))
        return jnp.concatenate(halves, axis=2)

    maps = strip(4, 7)
    decay = jnp.exp(-4.0 * layer.astype(jnp.float32) / Z)
    strips = steps_of(
        maps[:, 0:1],
        [maps[:, 1:2], maps[:, 2:3]],
        strip(0, 2),
        strip(2, 4),
        trace_strip,
        decay,
        shifts,
        masks,
    )
    edge = (lanes((1, X, C)) < 4) | (lanes((1, X, C)) >= C - 4)
    edge4 = (lanes((1, 4, C)) < 4) | (lanes((1, 4, C)) >= C - 4)
    for f in range(2):
        merged = jnp.where(inner[0], strips[1][f][1], strips[1][f][0])
        early = jnp.where(inner[0], strips[0][f][1], strips[0][f][0])
        for j in range(8):
            back = roll_last(merged, -(16 * j + 8))
            back_early = roll_last(early, -(16 * j + 8))
            for h in range(2):
                z = 8 * h + j
                value = jnp.where(edge[0], back[h], of_ref[f, z])
                of_ref[f, z] = value
                op_ref[1, f, z, 0:2, :] = value[0:2]
                op_ref[1, f, z, 2:4, :] = value[14:16]
                op_ref[0, f, z, 0:2, :] = jnp.where(edge4[0, 0:2], back_early[h, 0:2], op_ref[0, f, z, 0:2, :])
                op_ref[0, f, z, 2:4, :] = jnp.where(edge4[0, 0:2], back_early[h, 14:16], op_ref[0, f, z, 2:4, :])

    for i, offset in enumerate(ALL):

        @pl.when(exists(offset))
        def _(i=i, offset=offset):
            copy_of(i, offset).wait_send()


def solution(mesh):
    n_gx = mesh.shape["gx"]
    n_gy = mesh.shape["gy"]

    def shards(fields, phase, electrode, planes):
        in_hbm = pl.BlockSpec(memory_space=pltpu.HBM)
        vmem = pl.BlockSpec(memory_space=pltpu.VMEM)
        return pl.pallas_call(
            functools.partial(kernel, n_gx, n_gy),
            out_shape=(
                jax.ShapeDtypeStruct((2, Z, X, C), jnp.float32),
                jax.ShapeDtypeStruct((2, 2, Z, 4, C), jnp.float32),
            ),
            in_specs=[in_hbm] * 4,
            out_specs=(vmem, vmem),
            scratch_shapes=[
                pltpu.VMEM((2, Z, X, C), jnp.bfloat16),
                pltpu.VMEM((X, C), jnp.int32),
                pltpu.VMEM((2, X, C), jnp.int32),
                pltpu.VMEM((2, 2, Z, 4, C), jnp.float32),
                pltpu.VMEM((7, X, C), jnp.float32),
                pltpu.VMEM((2, 72, C), jnp.float32),
                pltpu.VMEM((2, 7, X, C), jnp.float32),
                pltpu.VMEM((2, 72, C), jnp.float32),
                pltpu.VMEM((4, 8, C), jnp.float32),
                pltpu.SemaphoreType.DMA((4,)),
                pltpu.SemaphoreType.DMA((8,)),
                pltpu.SemaphoreType.DMA((8,)),
            ],
            compiler_params=pltpu.CompilerParams(
                collective_id=0, has_side_effects=True, vmem_limit_bytes=32 * 1024 * 1024
            ),
        )(*[pltpu.with_memory_space_constraint(v, pltpu.HBM) for v in (fields, phase, electrode, planes)])

    placed = (
        P(None, None, "gx", "gy"),
        P("gx", "gy"),
        P(None, "gx", "gy"),
        P(None, None, None, "gx", "gy"),
    )
    return jax.shard_map(
        shards,
        mesh=mesh,
        in_specs=placed,
        out_specs=(P(None, None, "gx", "gy"), P(None, None, None, "gx", "gy")),
        check_vma=False,
    )
```

time: 74.2 us -> 11.3 us (0.15)
  the two profiles are of different devices: /device:TPU:24 before, /device:TPU:57 now
where the time goes in v1:
time: 11.3 us; the launch traced here: 11.2 us
  Pallas kernels  9.15 us (81%)
  local copies, waits for them, and re-layouts  1.36 us (12%)
  between operations  0.64 us (6%)
    pallas_call x1, Pallas kernels, shards(): pl.pallas_call(functools.partial(kernel, n_gx, n_gy), out_shape=(jax.Shap...  9.15 us
    unnamed x2, local copies, waits for them, and re-layouts  1.36 us

profile of v1, /device:TPU:57, one launch (start us, length us, event | category | flops | bytes accessed | tf_op | source)
XLA Modules:
  0.0 11.2 jit_solution(17939037988779999498)
XLA Ops:
  0.6 9.2 %shard_map.59 = (f32[2,16,16,128]{3,2,1,0:T(8,128)S(1)}, f32[2,2,16,4,128]{4,3,2,1,0:T(4,128)S(1)}) custom-call(bf16[2,16,16,128]{3,2,1,0:T(8,128)(2,1)} %f_hbm.1, s32[16,128]{1,0:T(8,128)} %ph_hbm.1, s32[2,16,128]{2,1,0:T(8,128)} %el_hbm.1, f32[2,2,16,4,128]{4,3,2,1,0:T(4,128)} %pl_hbm.1), custom_call_target="tpu_custom_call" | custom-call | tf_op jit(solution)/shard_map/pallas_call | solution.py:391
  9.8 0.7 %copy.8 = f32[2,16,16,128]{3,2,1,0:T(8,128)} copy(f32[2,16,16,128]{3,2,1,0:T(8,128)S(1)} %get-tuple-element.4) | data formatting | bytes 524288
  10.5 0.7 %copy.9 = f32[2,2,16,4,128]{4,3,2,1,0:T(4,128)} copy(f32[2,2,16,4,128]{4,3,2,1,0:T(4,128)S(1)} %get-tuple-element.5) | data formatting | bytes 262144

commit v2 on v1

--- a/solution.py
+++ b/solution.py
@@ -65,7 +65,7 @@
     return base + roll_last(base, 64)
 
 
-def steps_of(droplet, active, old_t, old_n, trace, decay, shifts, masks):
+def steps_of(droplet, active, old_t, old_n, decay, shifts, masks):
     xp, xm, yp, ym, zp, zm = shifts
     mxp, mxm, myp, mym, mzp, mzm, edge4 = masks
 
@@ -91,20 +91,27 @@
     heat = jnp.broadcast_to(cond_oil + (cond_drop - cond_oil) * droplet, old_t.shape)
     ion_base = diff_oil + (diff_drop - diff_oil) * droplet
     heat_faces, heat_robin, heat_inv = coefficients(heat)
-    states = []
-    for step in range(2):
+    def open_step(step, old_t, old_n):
         ions = ion_base * jnp.exp(thermal_slope * old_t)
-        source = (active[step] * droplet) * decay * (1.0 + 0.5 * old_n * old_n)
-        target_t = old_t + source + heat_robin * trace(step, 0)
-        first = sweep(old_t, target_t, heat_faces) * heat_inv
-        new_t = sweep(first, target_t, heat_faces) * (take_new * heat_inv) - keep_old * old_t
+        target_t = old_t + (active[step] * droplet) * decay * (1.0 + 0.5 * old_n * old_n)
         ion_faces, ion_robin, ion_inv = coefficients(ions)
-        target_n = old_n + ion_robin * trace(step, 1)
-        first = sweep(old_n, target_n, ion_faces) * ion_inv
-        new_n = sweep(first, target_n, ion_faces) * (take_new * ion_inv) - keep_old * old_n
-        old_t, old_n = new_t, new_n
-        states.append((old_t, old_n))
-    return states
+        return (
+            (old_t, target_t, sweep(old_t, target_t, heat_faces), heat_faces, heat_robin, heat_inv),
+            (old_n, old_n, sweep(old_n, old_n, ion_faces), ion_faces, ion_robin, ion_inv),
+        )
+
+    def close_step(parts, step, trace):
+        out = []
+        for field, (old, target, total, faces, robin, inv) in enumerate(parts):
+            given = robin * trace(step, field)
+            first = (total + given) * inv
+            out.append(sweep(first, target + given, faces) * (take_new * inv) - keep_old * old)
+        return out
+
+    parts = open_step(0, old_t, old_n)
+    trace = yield
+    early = close_step(parts, 0, trace)
+    yield early, close_step(open_step(1, *early), 1, trace)
 
 
 def kernel(
@@ -237,9 +244,6 @@
         def _():
             copy_of(ALL.index(back), back).wait_recv()
 
-    for offset in SIDES_X:
-        wait_from(offset)
-
     rows = row_masks(3)
     layer = lax.broadcasted_iota(jnp.int32, (Z, 1, 1), 0)
     one = jnp.float32(1.0)
@@ -269,22 +273,25 @@
 
     decay = jnp.exp(-4.0 * layer.astype(jnp.float32) / Z)
     active = [el_in[s].astype(jnp.float32)[None] for s in range(2)]
-    states = steps_of(
+    work = steps_of(
         ph_in[...].astype(jnp.float32)[None],
         active,
         f_in[0].astype(jnp.float32),
         f_in[1].astype(jnp.float32),
-        trace_own,
         decay,
         shifts,
         masks,
     )
+    next(work)
+    for offset in SIDES_X:
+        wait_from(offset)
+    states = work.send(trace_own)
     for f in range(2):
         op_ref[0, f, :, 0:2, :] = states[0][f][:, 0:2, :]
         op_ref[0, f, :, 2:4, :] = states[0][f][:, 14:16, :]
         of_ref[f] = states[1][f]
 
-    for offset in SIDES_Y + CORNERS:
+    for offset in SIDES_Y:
         wait_from(offset)
 
     lane = lanes((1, 1, 1, C))
@@ -347,16 +354,19 @@
 
     maps = strip(4, 7)
     decay = jnp.exp(-4.0 * layer.astype(jnp.float32) / Z)
-    strips = steps_of(
+    work = steps_of(
         maps[:, 0:1],
         [maps[:, 1:2], maps[:, 2:3]],
         strip(0, 2),
         strip(2, 4),
-        trace_strip,
         decay,
         shifts,
         masks,
     )
+    next(work)
+    for offset in CORNERS:
+        wait_from(offset)
+    strips = work.send(trace_strip)
     edge = (lanes((1, X, C)) < 4) | (lanes((1, X, C)) >= C - 4)
     edge4 = (lanes((1, 4, C)) < 4) | (lanes((1, 4, C)) >= C - 4)
     for f in range(2):
@@ -381,6 +391,17 @@
             copy_of(i, offset).wait_send()
 
 
+def write_out(f_ref, p_ref, of_hbm, op_hbm, sem):
+    copies = [
+        pltpu.make_async_copy(f_ref, of_hbm, sem.at[0]),
+        pltpu.make_async_copy(p_ref, op_hbm, sem.at[1]),
+    ]
+    for copy in copies:
+        copy.start()
+    for copy in copies:
+        copy.wait()
+
+
 def solution(mesh):
     n_gx = mesh.shape["gx"]
     n_gy = mesh.shape["gy"]
@@ -388,7 +409,7 @@
     def shards(fields, phase, electrode, planes):
         in_hbm = pl.BlockSpec(memory_space=pltpu.HBM)
         vmem = pl.BlockSpec(memory_space=pltpu.VMEM)
-        return pl.pallas_call(
+        made = pl.pallas_call(
             functools.partial(kernel, n_gx, n_gy),
             out_shape=(
                 jax.ShapeDtypeStruct((2, Z, X, C), jnp.float32),
@@ -414,6 +435,16 @@
                 collective_id=0, has_side_effects=True, vmem_limit_bytes=32 * 1024 * 1024
             ),
         )(*[pltpu.with_memory_space_constraint(v, pltpu.HBM) for v in (fields, phase, electrode, planes)])
+        return pl.pallas_call(
+            write_out,
+            out_shape=(
+                pltpu.HBM((2, Z, X, C), jnp.float32),
+                pltpu.HBM((2, 2, Z, 4, C), jnp.float32),
+            ),
+            in_specs=[vmem, vmem],
+            out_specs=(in_hbm, in_hbm),
+            scratch_shapes=[pltpu.SemaphoreType.DMA((2,))],
+        )(*[pltpu.with_memory_space_constraint(v, pltpu.VMEM) for v in made])
 
     placed = (
         P(None, None, "gx", "gy"),

time: 11.3 us -> 10.3 us (0.912)
  local copies, waits for them, and re-layouts: 1.36 us -> 0 us
  Pallas kernels: 9.15 us -> 9.51 us
    unnamed x2 -> x0, local copies, waits for them, and re-layouts: 1.36 us -> none
    pallas_call x0 -> x1, Pallas kernels: none -> 0.76 us  [shards(): pl.pallas_call(write_out, out_shape=(pltpu.HBM((2, Z, X, C), jnp.float32)...]
    pallas_call x1, Pallas kernels: 9.15 us -> 8.75 us  [shards(): pl.pallas_call(functools.partial(kernel, n_gx, n_gy), out_shape=(jax.Shap...]
where the time goes in v2:
time: 10.3 us; the launch traced here: 10.1 us
  Pallas kernels  9.51 us (92%)
  between operations  0.64 us (6%)
    pallas_call x1, Pallas kernels, shards(): pl.pallas_call(functools.partial(kernel, n_gx, n_gy), out_shape=(jax.Shap...  8.75 us
    pallas_call x1, Pallas kernels, shards(): pl.pallas_call(write_out, out_shape=(pltpu.HBM((2, Z, X, C), jnp.float32)...  0.76 us

profile of v2, /device:TPU:57, one launch (start us, length us, event | category | flops | bytes accessed | tf_op | source)
XLA Modules:
  0.0 10.1 jit_solution(16755970806009483742)
XLA Ops:
  0.6 8.7 %shard_map.59 = (f32[2,16,16,128]{3,2,1,0:T(8,128)S(1)}, f32[2,2,16,4,128]{4,3,2,1,0:T(4,128)S(1)}) custom-call(bf16[2,16,16,128]{3,2,1,0:T(8,128)(2,1)} %f_hbm.1, s32[16,128]{1,0:T(8,128)} %ph_hbm.1, s32[2,16,128]{2,1,0:T(8,128)} %el_hbm.1, f32[2,2,16,4,128]{4,3,2,1,0:T(4,128)} %pl_hbm.1), custom_call_target="tpu_custom_call" | custom-call | tf_op jit(solution)/shard_map/pallas_call | solution.py:412
  9.4 0.8 %shard_map.60 = (f32[2,16,16,128]{3,2,1,0:T(8,128)}, f32[2,2,16,4,128]{4,3,2,1,0:T(4,128)}) custom-call(f32[2,16,16,128]{3,2,1,0:T(8,128)S(1)} %get-tuple-element.4.f_ref, f32[2,2,16,4,128]{4,3,2,1,0:T(4,128)S(1)} %get-tuple-element.5.p_ref), custom_call_target="tpu_custom_call" | custom-call | tf_op jit(solution)/shard_map/pallas_call | solution.py:438

commit v3 on v2

v3 whole, which is shorter than its diff:
```python
import functools

import jax
import jax.numpy as jnp
from jax import lax
from jax.experimental import pallas as pl
from jax.experimental.pallas import tpu as pltpu
from jax.sharding import PartitionSpec as P

MESH = pl.DeviceIdType.MESH
cond_oil = 0.6
cond_drop = 2.0
diff_oil = 0.3
diff_drop = 1.0
thermal_slope = 0.3
cheb_radius = 0.95
cheb_ratio = 1.0 / cheb_radius
rho_first = 1.0 / cheb_ratio
rho_second = 1.0 / (2.0 * cheb_ratio - rho_first)
log2_e = 1.4426950408889634
keep_old = rho_second * rho_first
take_new = 2.0 * rho_second / cheb_radius

Z = 16
X = 16
C = 128
CORNERS = ((-1, -1), (-1, 1), (1, -1), (1, 1))
SIDES_Y = ((0, -1), (0, 1))
SIDES_X = ((-1, 0), (1, 0))
ALL = CORNERS + SIDES_Y + SIDES_X


def lanes(shape):
    return lax.broadcasted_iota(jnp.int32, shape, len(shape) - 1)


def roll_last(v, shift):
    return pltpu.roll(v, shift % C, v.ndim - 1)


def roll_rows(v, shift):
    return pltpu.roll(v, shift % X, v.ndim - 2)


def row_masks(ndim):
    shape = (1,) * (ndim - 2) + (X, C)
    rows = lax.broadcasted_iota(jnp.int32, shape, ndim - 2)
    return rows


def packed_columns(v):
    head = v.shape[:-3]
    v = v.reshape(head + (2, 8, X, C))
    lane = lanes(head + (2, X, C))
    out = None
    for j in range(8):
        moved = roll_last(v[..., j, :, :], 16 * j + 8)
        out = moved if out is None else jnp.where(lane >= 16 * j, moved, out)
    return out


def packed_map(v):
    base = jnp.where(lanes(v.shape) < 16, roll_last(v, 8), 0.0)
    base = base + roll_last(base, 16)
    base = base + roll_last(base, 32)
    return base + roll_last(base, 64)


def periodic_columns(v):
    base = jnp.where(lanes(v.shape) < 8, roll_last(v, 4), 0.0)
    for shift in (8, 16, 32, 64):
        base = base + roll_last(base, shift)
    return base


def edge_columns(v):
    lane = lanes(v.shape[:-3] + (X, C))
    out = None
    for z in range(Z):
        moved = roll_last(v[..., z, :, :], 8 * z + 4)
        out = moved if out is None else jnp.where(lane >= 8 * z, moved, out)
    return out


def wider(v):
    v = jnp.stack([roll_last(v, 4), roll_last(v, -60)], axis=v.ndim - 2)
    lane = lanes(v.shape)
    v = jnp.where(lane >= 64, roll_last(v, 32), v)
    v = jnp.where(lane % 64 >= 32, roll_last(v, 16), v)
    return jnp.where(lane % 32 >= 16, roll_last(v, 8), v)


def inverse(v):
    guess = pl.reciprocal(v, approx=True)
    return guess * (2.0 - v * guess)


def steps_of(droplet, active, old_t, old_n, decay, grid):
    def sweep(v, target, faces):
        px, mx, py, my, z_part = faces
        along = px * grid.xp(v) + mx * grid.xm(v)
        across = py * grid.yp(v) + my * grid.ym(v)
        return (target + along) + (across + z_part(v))

    def sides(k):
        px = grid.x_closed(k + grid.xp(k))
        py = grid.y_closed(k + grid.yp(k))
        return px, grid.xm(px), py, grid.ym(py)

    def coefficients(k):
        px, mx, py, my = sides(k)
        z_part, z_total = grid.layers(k)
        robin = k * grid.edge4
        diagonal = (1.0 + robin) + (px + mx) + (py + my) + z_total
        return (px, mx, py, my, z_part), robin, inverse(diagonal)

    def heat_coefficients(k):
        px, mx, py, my = sides(k)
        robin = k * grid.edge4
        diagonal = (1.0 + robin) + (px + mx) + (py + my)
        z_part, inv = grid.even_layers(k, diagonal)
        return (px, mx, py, my, z_part), robin, inv

    ion_base = diff_oil + (diff_drop - diff_oil) * droplet
    heat_faces, heat_robin, heat_inv = heat_coefficients(cond_oil + (cond_drop - cond_oil) * droplet)
    heating = [(0.5 * (e * droplet)) * decay for e in active]

    def open_step(step, old_t, old_n):
        ions = ion_base * jnp.exp2((thermal_slope * log2_e) * old_t)
        target_t = old_t + heating[step] * (2.0 + old_n * old_n)
        ion_faces, ion_robin, ion_inv = coefficients(ions)
        return (
            (old_t, target_t, sweep(old_t, target_t, heat_faces), heat_faces, heat_robin, heat_inv),
            (old_n, old_n, sweep(old_n, old_n, ion_faces), ion_faces, ion_robin, ion_inv),
        )

    def close_step(parts, step, trace):
        out = []
        for field, (old, target, total, faces, robin, inv) in enumerate(parts):
            given = robin * trace(step, field)
            first = (total + given) * inv
            out.append(sweep(first, target + given, faces) * (take_new * inv) - keep_old * old)
        return out

    parts = open_step(0, old_t, old_n)
    trace = yield
    early = close_step(parts, 0, trace)
    yield early, close_step(open_step(1, *early), 1, trace)


class Rolled:
    def xp(self, v):
        return roll_rows(v, -1)

    def xm(self, v):
        return roll_rows(v, 1)

    def yp(self, v):
        return roll_last(v, -1)

    def ym(self, v):
        return roll_last(v, 1)

    def x_closed(self, face):
        half = face[..., 8:, :]
        rows = lax.broadcasted_iota(jnp.int32, (1,) * (face.ndim - 2) + (8, C), face.ndim - 2)
        return jnp.concatenate([face[..., :8, :], jnp.where(rows == 7, 0.0, half)], axis=face.ndim - 2)


class Span:
    def __init__(self, values, start):
        self.values, self.start = values, start

    def __call__(self, lo, hi):
        return self.values[lo - self.start : hi - self.start]


def gathered(function, lo, hi, size=4):
    return Span(jnp.concatenate([function(a, min(a + size, hi)) for a in range(lo, hi, size)], axis=0), lo)


def joined(*spans):
    return Span(jnp.concatenate([span.values for span in spans], axis=0), spans[0].start)


def x_sum(face, v, lo, hi):
    top, low = min(hi, X - 1), max(lo - 1, 0)
    up = face(lo, top)
    down = face(low, hi - 1)
    if v is not None:
        up = up * v(lo + 1, top + 1)
        down = down * v(low, hi - 1)
    first, last = max(lo, 1), top
    parts = [up[:1]] if lo == 0 else []
    if last > first:
        parts.append(up[first - lo : last - lo] + down[first - low - 1 : last - low - 1])
    if hi == X:
        parts.append(down[-1:])
    return jnp.concatenate(parts, axis=0)


class OwnColumns:
    def __init__(self, droplet, active, temper, ions, decay):
        self.olds = [[Span(temper, 0), Span(ions, 0)]]
        both = lambda v: jnp.concatenate([v, v], axis=1)
        heat = cond_oil + (cond_drop - cond_oil) * droplet
        self.ion_base = both(diff_oil + (diff_drop - diff_oil) * droplet)
        self.heating = [Span(both(0.5 * (e * droplet)) * decay, 0) for e in active]
        face = Span(heat[1:] + heat[:-1], 0)
        py = heat + roll_last(heat, -1)
        my = roll_last(py, 1)
        edge = jnp.concatenate([heat[:1], jnp.zeros_like(heat[1:-1]), heat[-1:]], axis=0)
        base = (1.0 + 4.0 * edge) + x_sum(face, None, 0, X) + (py + my)
        twice = both(2.0 * heat)
        row = lax.broadcasted_iota(jnp.int32, (1, Z, C), 1)
        pz = jnp.where(row == Z - 1, 0.0, twice)
        mz = jnp.where(row == 0, 0.0, twice)
        heat_faces = (Span(both(face.values), 0), Span(both(py), 0), Span(both(my), 0), Span(pz, 0), Span(mz, 0))
        self.heat = (heat_faces, Span(inverse(both(base) + (pz + mz)), 0), Span(both(heat), 0))
        self.states = []

    def ion_parts(self, temper, lo, hi):
        k = self.ion_base[lo:hi] * jnp.exp2((thermal_slope * log2_e) * temper(lo, hi))
        py = k + roll_last(k, -1)
        row = lax.broadcasted_iota(jnp.int32, (1, 8, C), 1)
        pz = k + roll_rows(k, -1)
        pz = jnp.concatenate([pz[:, :8], jnp.where(row == 7, 0.0, pz[:, 8:])], axis=1)
        return k, py, roll_last(py, 1), pz, roll_rows(pz, 1)

    def ion_spans(self, temper, lo, hi):
        parts = [self.ion_parts(temper, a, min(a + 4, hi)) for a in range(lo, hi, 4)]
        return [Span(jnp.concatenate(p, axis=0), lo) for p in zip(*parts)]

    def ion_inverse(self, spans, face, lo, hi):
        def part(a, b):
            k, py, my, pz, mz = [v(a, b) for v in spans]
            total = (1.0 + x_sum(face, None, a, b)) + (py + my) + (pz + mz)
            if a == 0:
                total = jnp.concatenate([total[:1] + 4.0 * k[:1], total[1:]], axis=0)
            if b == X:
                total = jnp.concatenate([total[:-1], total[-1:] + 4.0 * k[-1:]], axis=0)
            return inverse(total)

        return gathered(part, lo, hi)

    def sweep(self, v, target, faces, a, b):
        face, py, my, pz, mz = faces
        mid = v(a, b)
        across = py(a, b) * roll_last(mid, -1) + my(a, b) * roll_last(mid, 1)
        upright = pz(a, b) * roll_rows(mid, -1) + mz(a, b) * roll_rows(mid, 1)
        return (target(a, b) + x_sum(face, v, a, b)) + (across + upright)

    def targets(self, step, old, lo, hi):
        heated = lambda a, b: old[0](a, b) + self.heating[step](a, b) * (2.0 + old[1](a, b) * old[1](a, b))
        return [gathered(heated, lo, hi), Span(old[1](lo, hi), lo)]

    def last(self, old, target, first, faces, inv, lo, hi):
        def part(a, b):
            return self.sweep(first, target, faces, a, b) * (take_new * inv(a, b)) - keep_old * old(a, b)

        return gathered(part, lo, hi)

    def before(self):
        old = self.olds[0]
        spans = self.ion_spans(old[0], 0, X)
        face = Span(spans[0].values[1:] + spans[0].values[:-1], 0)
        ion = ((face, *spans[1:]), self.ion_inverse(spans, face, 0, X), spans[0])
        self.sets0 = (self.heat, ion)
        self.target0 = self.targets(0, old, 0, X)
        self.total0, self.first0, self.mid1 = [], [], []
        for f in range(2):
            faces, inv, k = self.sets0[f]
            total = gathered(lambda a, b: self.sweep(old[f], self.target0[f], faces, a, b), 0, X)
            first = gathered(lambda a, b: total(a, b) * inv(a, b), 1, X - 1)
            self.total0.append(total)
            self.first0.append(first)
            self.mid1.append(self.last(old[f], self.target0[f], first, faces, inv, 2, X - 2))
        new = self.mid1
        self.spans1 = self.ion_spans(new[0], 2, X - 2)
        k = self.spans1[0]
        self.face1 = Span(k.values[1:] + k.values[:-1], 2)
        self.inv1 = self.ion_inverse(self.spans1, self.face1, 3, X - 3)
        self.target1 = self.targets(1, new, 2, X - 2)
        sets = ((self.heat[0], self.heat[1]), ((self.face1, *self.spans1[1:]), self.inv1))
        self.first1, self.mid2 = [], []
        for f in range(2):
            faces, inv = sets[f]
            first = gathered(lambda a, b: self.sweep(new[f], self.target1[f], faces, a, b) * inv(a, b), 3, X - 3)
            self.first1.append(first)
            self.mid2.append(self.last(new[f], self.target1[f], first, faces, inv, 4, X - 4))

    def after(self, trace):
        old = self.olds[0]
        news = []
        for f in range(2):
            faces, inv, k = self.sets0[f]
            ends, target = [], self.target0[f].values
            for side, x in ((0, 0), (1, X - 1)):
                given = 4.0 * k(x, x + 1) * trace(0, f, side)
                ends.append((self.total0[f](x, x + 1) + given) * inv(x, x + 1))
                target = (
                    jnp.concatenate([target[:1] + given, target[1:]], axis=0)
                    if side == 0
                    else jnp.concatenate([target[:-1], target[-1:] + given], axis=0)
                )
            first = Span(jnp.concatenate([ends[0], self.first0[f].values, ends[1]], axis=0), 0)
            target = Span(target, 0)
            low = self.last(old[f], target, first, faces, inv, 0, 2)
            high = self.last(old[f], target, first, faces, inv, X - 2, X)
            news.append(joined(low, self.mid1[f], high))
        low, high = self.ion_spans(news[0], 0, 2), self.ion_spans(news[0], X - 2, X)
        spans = [joined(a, b, c) for a, b, c in zip(low, self.spans1, high)]
        k = spans[0].values
        face = Span(
            jnp.concatenate([k[1:3] + k[0:2], self.face1.values, k[X - 2 :] + k[X - 3 : X - 1]], axis=0), 0
        )
        inv = joined(self.ion_inverse(spans, face, 0, 3), self.inv1, self.ion_inverse(spans, face, X - 3, X))
        low, high = self.targets(1, news, 0, 2), self.targets(1, news, X - 2, X)
        ends = []
        for f, (faces, inv, k) in enumerate((self.heat, ((face, *spans[1:]), inv, spans[0]))):
            target = joined(low[f], self.target1[f], high[f]).values
            target = Span(
                jnp.concatenate(
                    [
                        target[:1] + 4.0 * k(0, 1) * trace(1, f, 0),
                        target[1:-1],
                        target[-1:] + 4.0 * k(X - 1, X) * trace(1, f, 1),
                    ],
                    axis=0,
                ),
                0,
            )
            part = lambda a, b: self.sweep(news[f], target, faces, a, b) * inv(a, b)
            first = joined(gathered(part, 0, 3), self.first1[f], gathered(part, X - 3, X))
            ends.append(
                joined(
                    self.last(news[f], target, first, faces, inv, 0, 4),
                    self.mid2[f],
                    self.last(news[f], target, first, faces, inv, X - 4, X),
                )
            )
        return news, ends


class Strips(Rolled):
    def __init__(self, left_open, right_open):
        rows = row_masks(4)
        self.lane = lanes((1, 1, 1, C))
        self.column = self.lane % 16
        layer = 8 * lax.broadcasted_iota(jnp.int32, (1, 2, 1, 1), 1) + self.lane // 16
        side = lax.broadcasted_iota(jnp.int32, (2, 1, 1, 1), 0)
        self.edge4 = jnp.where((rows == 0) | (rows == X - 1), 4.0, 0.0)
        self.between = jnp.where(self.column == 7, jnp.where(side == 0, left_open, right_open), 1.0)
        self.below_top = (layer < Z - 1).astype(jnp.float32)
        self.decay = jnp.exp(-4.0 * layer.astype(jnp.float32) / Z)

    def y_closed(self, face):
        return face * self.between

    def zp(self, v):
        moved = roll_last(v, -16)
        return jnp.where(self.lane < 112, moved, jnp.concatenate([moved[:, 1:2], moved[:, 0:1]], axis=1))

    def zm(self, v):
        moved = roll_last(v, 16)
        return jnp.where(self.lane >= 16, moved, jnp.concatenate([moved[:, 1:2], moved[:, 0:1]], axis=1))

    def layers(self, k):
        up = (k + self.zp(k)) * self.below_top
        down = self.zm(up)
        return lambda v: up * self.zp(v) + down * self.zm(v), up + down

    def even_layers(self, k, diagonal):
        up = jnp.broadcast_to(2.0 * k, k.shape[:1] + (2,) + k.shape[2:]) * self.below_top
        down = self.zm(up)
        return lambda v: up * self.zp(v) + down * self.zm(v), inverse(diagonal + (up + down))


def kernel(
    n_gx,
    n_gy,
    f_hbm,
    ph_hbm,
    el_hbm,
    pl_hbm,
    of_ref,
    op_ref,
    f_in,
    f_32,
    ph_in,
    el_in,
    pl_in,
    own_b,
    send_b,
    send_g,
    recv_b,
    recv_g,
    recv_c,
    in_sem,
    send_sem,
    recv_sem,
):
    gx = lax.axis_index("gx")
    gy = lax.axis_index("gy")

    def exists(offset):
        found = []
        for place, move, count in ((gx, offset[0], n_gx), (gy, offset[1], n_gy)):
            if move < 0:
                found.append(place > 0)
            if move > 0:
                found.append(place < count - 1)
        return functools.reduce(jnp.logical_and, found)

    def at(offset):
        return (gx + offset[0], gy + offset[1])

    barrier = pltpu.get_barrier_semaphore()
    expected = jnp.int32(0)
    for offset in ALL:

        @pl.when(exists(offset))
        def _(offset=offset):
            pl.semaphore_signal(barrier, inc=1, device_id=at(offset), device_id_type=MESH)

        expected = expected + exists(offset).astype(jnp.int32)

    loads = [
        pltpu.make_async_copy(src, dst, in_sem.at[i])
        for i, (src, dst) in enumerate(((ph_hbm, ph_in), (el_hbm, el_in), (f_hbm, f_in), (pl_hbm, pl_in)))
    ]
    for load in loads:
        load.start()

    for i, offset in enumerate(SIDES_Y):

        @pl.when(jnp.logical_not(exists(offset)))
        def _(i=i):
            recv_b[i] = jnp.zeros(recv_b.shape[1:], jnp.float32)

    for i, offset in enumerate(SIDES_X):

        @pl.when(jnp.logical_not(exists(offset)))
        def _(i=i):
            recv_g[i] = jnp.zeros(recv_g.shape[1:], jnp.float32)

    for i, offset in enumerate(CORNERS):

        @pl.when(jnp.logical_not(exists(offset)))
        def _(i=i):
            recv_c[i] = jnp.zeros(recv_c.shape[1:], jnp.float32)

    for load in loads:
        load.wait()
    maps = [ph_in[...].astype(jnp.float32), el_in[0].astype(jnp.float32), el_in[1].astype(jnp.float32)]
    drop, on0, on1 = [periodic_columns(m) for m in maps]
    near = edge_columns(f_in[...].astype(jnp.float32))
    place = lanes((X, C)) % 8
    send_b[0, 0] = jnp.where(place >= 4, near[0], roll_last(drop, -4))
    send_b[0, 1] = jnp.where(place >= 4, near[1], jnp.where(place == 0, roll_last(on1, -4), roll_last(on0, -3)))
    send_b[1, 0] = jnp.where(place < 4, near[0], roll_last(drop, 4))
    send_b[1, 1] = jnp.where(place < 4, near[1], jnp.where(place == 7, roll_last(on1, 4), roll_last(on0, 3)))
    own_row = lax.broadcasted_iota(jnp.int32, (Z, C), 0) % 8 == lanes((Z, C)) // 16
    for side in range(2):
        near, far = ((0, 1), (3, 2))[side]
        for s in range(2):
            for f in range(2):
                a = pl_in[s, f, :, near, :]
                b = pl_in[s, f, :, far, :]
                g = a + 0.5 * (a - b)
                row = (s * 2 + f) * Z
                send_g[side, row : row + Z, :] = g
                spread = pltpu.roll(g, 8, 1, stride=16, stride_axis=0)
                spread = jnp.where(own_row, spread, 0.0).reshape(2, 8, C)
                row = 64 + (s * 2 + f) * 2
                send_g[side, row : row + 2, :] = jnp.sum(spread, axis=1)

    pl.semaphore_wait(barrier, expected)

    def copy_of(i, offset):
        back = (-offset[0], -offset[1])
        if offset in CORNERS:
            src = send_g.at[(offset[0] + 1) // 2, pl.ds(64, 8)]
            dst = recv_c.at[CORNERS.index(back)]
        elif offset in SIDES_Y:
            src = send_b.at[(offset[1] + 1) // 2]
            dst = recv_b.at[SIDES_Y.index(back)]
        else:
            src = send_g.at[(offset[0] + 1) // 2]
            dst = recv_g.at[SIDES_X.index(back)]
        return pltpu.make_async_remote_copy(
            src_ref=src,
            dst_ref=dst,
            send_sem=send_sem.at[i],
            recv_sem=recv_sem.at[ALL.index(back)],
            device_id=at(offset),
            device_id_type=MESH,
        )

    for i, offset in enumerate(ALL):

        @pl.when(exists(offset))
        def _(i=i, offset=offset):
            copy_of(i, offset).start()

    for i in range(3):
        own_b[4 + i] = packed_map(maps[i])
    own_b[0:4] = packed_columns(f_in[...].astype(jnp.float32)).reshape(4, X, C)

    def wait_from(offset):
        back = (-offset[0], -offset[1])

        @pl.when(exists(offset))
        def _():
            copy_of(ALL.index(back), back).wait_recv()

    for f in range(2):
        f_32[f] = f_in[f].astype(jnp.float32).reshape(Z * X, C)
    planes_x = lambda f: jnp.stack([f_32[f, pl.ds(x, Z, stride=X), :] for x in range(X)], axis=0)
    rows = lambda v: jnp.broadcast_to(v[:, None, :], (X, 8, C))
    height = lax.broadcasted_iota(jnp.int32, (1, Z, C), 1)
    decay = jnp.exp(-4.0 * height.astype(jnp.float32) / Z)
    columns = OwnColumns(rows(maps[0]), [rows(maps[1]), rows(maps[2])], planes_x(0), planes_x(1), decay)
    columns.before()
    for offset in SIDES_X + SIDES_Y:
        wait_from(offset)

    def trace_own(step, field, side):
        row = (step * 2 + field) * Z
        return recv_g[side, row : row + Z, :][None]

    early, late = columns.after(trace_own)
    for f in range(2):
        for x in range(X):
            of_ref[f, pl.ds(x, Z, stride=X), :] = late[f].values[x]
        for p, x in enumerate((0, 1, X - 2, X - 1)):
            op_ref[0, f, pl.ds(p, Z, stride=4), :] = early[f].values[x]

    grid = Strips((gy > 0).astype(jnp.float32), (gy < n_gy - 1).astype(jnp.float32))
    inner = grid.column < 8

    def strip(outer, own):
        inside = inner[0, 0]
        return jnp.stack([jnp.where(inside, outer[0], own), jnp.where(inside, own, outer[1])], axis=0)

    def trace_strip(step, field):
        row = (step * 2 + field) * 2
        halves = []
        for i in range(2):
            mid = recv_g[i, 64 + row : 66 + row, :]
            low = jnp.where(inner[0, 0], recv_c[2 * i, row : row + 2, :], mid)
            high = jnp.where(inner[0, 0], mid, recv_c[2 * i + 1, row : row + 2, :])
            both = jnp.stack([low, high], axis=0)[:, :, None, :]
            halves.append(jnp.broadcast_to(both, (2, 2, 8, C)))
        return jnp.concatenate(halves, axis=2)

    fields = [strip([wider(recv_b[i, f]) for i in range(2)], own_b[2 * f : 2 * f + 2]) for f in range(2)]
    drop = strip([recv_b[0, 0], recv_b[1, 0]], own_b[4])
    on0 = strip([roll_last(recv_b[0, 1], 1), roll_last(recv_b[1, 1], -1)], own_b[5])
    on1 = strip([recv_b[0, 1], recv_b[1, 1]], own_b[6])
    work = steps_of(
        drop[:, None],
        [on0[:, None], on1[:, None]],
        fields[0],
        fields[1],
        grid.decay,
        grid,
    )
    next(work)
    for offset in CORNERS:
        wait_from(offset)
    strips = work.send(trace_strip)
    lane = lanes((X, C))
    edge = (lane < 4) | (lane >= C - 4)

    def four(v):
        return [v[..., 0:2, :], v[..., X - 2 : X, :]]

    def both_sides(state):
        return jnp.where(inner[0], state[1], state[0])

    early = jnp.concatenate(four(both_sides(strips[0][0])) + four(both_sides(strips[0][1])), axis=1)
    for j in range(8):
        back = roll_last(early, -(16 * j + 8))
        for h in range(2):
            z = 8 * h + j
            for f in range(2):
                rows = slice(4 * z, 4 * z + 4)
                op_ref[0, f, rows, :] = jnp.where(edge[:4], back[h, 4 * f : 4 * f + 4], op_ref[0, f, rows, :])
    for f in range(2):
        merged = both_sides(strips[1][f])
        for j in range(8):
            back = roll_last(merged, -(16 * j + 8))
            for h in range(2):
                z = 8 * h + j
                rows = slice(X * z, X * z + X)
                value = jnp.where(edge, back[h], of_ref[f, rows, :])
                of_ref[f, rows, :] = value
                op_ref[1, f, 4 * z : 4 * z + 4, :] = jnp.concatenate(four(value), axis=0)

    for i, offset in enumerate(ALL):

        @pl.when(exists(offset))
        def _(i=i, offset=offset):
            copy_of(i, offset).wait_send()


def write_out(f_ref, p_ref, of_hbm, op_hbm, sem):
    copies = [
        pltpu.make_async_copy(f_ref, of_hbm, sem.at[0]),
        pltpu.make_async_copy(p_ref, op_hbm, sem.at[1]),
    ]
    for copy in copies:
        copy.start()
    for copy in copies:
        copy.wait()


def solution(mesh):
    n_gx = mesh.shape["gx"]
    n_gy = mesh.shape["gy"]

    def shards(fields, phase, electrode, planes):
        in_hbm = pl.BlockSpec(memory_space=pltpu.HBM)
        vmem = pl.BlockSpec(memory_space=pltpu.VMEM)
        made = pl.pallas_call(
            functools.partial(kernel, n_gx, n_gy),
            out_shape=(
                jax.ShapeDtypeStruct((2, Z * X, C), jnp.float32),
                jax.ShapeDtypeStruct((2, 2, Z * 4, C), jnp.float32),
            ),
            in_specs=[in_hbm] * 4,
            out_specs=(vmem, vmem),
            scratch_shapes=[
                pltpu.VMEM((2, Z, X, C), jnp.bfloat16),
                pltpu.VMEM((2, Z * X, C), jnp.float32),
                pltpu.VMEM((X, C), jnp.int32),
                pltpu.VMEM((2, X, C), jnp.int32),
                pltpu.VMEM((2, 2, Z, 4, C), jnp.float32),
                pltpu.VMEM((7, X, C), jnp.float32),
                pltpu.VMEM((2, 2, X, C), jnp.float32),
                pltpu.VMEM((2, 72, C), jnp.float32),
                pltpu.VMEM((2, 2, X, C), jnp.float32),
                pltpu.VMEM((2, 72, C), jnp.float32),
                pltpu.VMEM((4, 8, C), jnp.float32),
                pltpu.SemaphoreType.DMA((4,)),
                pltpu.SemaphoreType.DMA((8,)),
                pltpu.SemaphoreType.DMA((8,)),
            ],
            compiler_params=pltpu.CompilerParams(
                collective_id=0, has_side_effects=True, vmem_limit_bytes=32 * 1024 * 1024
            ),
        )(*[pltpu.with_memory_space_constraint(v, pltpu.HBM) for v in (fields, phase, electrode, planes)])
        new_fields, new_planes = pl.pallas_call(
            write_out,
            out_shape=(
                pltpu.HBM((2, Z * X, C), jnp.float32),
                pltpu.HBM((2, 2, Z * 4, C), jnp.float32),
            ),
            in_specs=[vmem, vmem],
            out_specs=(in_hbm, in_hbm),
            scratch_shapes=[pltpu.SemaphoreType.DMA((2,))],
        )(*[pltpu.with_memory_space_constraint(v, pltpu.VMEM) for v in made])
        return new_fields.reshape(2, Z, X, C), new_planes.reshape(2, 2, Z, 4, C)

    placed = (
        P(None, None, "gx", "gy"),
        P("gx", "gy"),
        P(None, "gx", "gy"),
        P(None, None, None, "gx", "gy"),
    )
    return jax.shard_map(
        shards,
        mesh=mesh,
        in_specs=placed,
        out_specs=(P(None, None, "gx", "gy"), P(None, None, None, "gx", "gy")),
        check_vma=False,
    )
```

time: 10.3 us -> 10.1 us (0.981)
  Pallas kernels: 9.51 us -> 9.32 us
    pallas_call x1, Pallas kernels: 8.75 us -> 8.56 us  [shards(): pl.pallas_call(functools.partial(kernel, n_gx, n_gy), out_shape=(jax.Shap...]
where the time goes in v3:
time: 10.1 us; the launch traced here: 9.96 us
  Pallas kernels  9.32 us (92%)
  between operations  0.64 us (6%)
    pallas_call x1, Pallas kernels, shards(): pl.pallas_call(functools.partial(kernel, n_gx, n_gy), out_shape=(jax.Shap...  8.56 us
    pallas_call x1, Pallas kernels, shards(): pl.pallas_call(write_out, out_shape=(pltpu.HBM((2, Z * X, C), jnp.float32...  0.76 us

profile of v3, /device:TPU:57, one launch (start us, length us, event | category | flops | bytes accessed | tf_op | source)
XLA Modules:
  0.0 10.0 jit_solution(10959182880787885668)
XLA Ops:
  0.6 8.6 %shard_map.59 = (f32[2,256,128]{2,1,0:T(8,128)S(1)}, f32[2,2,64,128]{3,2,1,0:T(8,128)S(1)}) custom-call(bf16[2,16,16,128]{3,2,1,0:T(8,128)(2,1)} %f_hbm.1, s32[16,128]{1,0:T(8,128)} %ph_hbm.1, s32[2,16,128]{2,1,0:T(8,128)} %el_hbm.1, f32[2,2,16,4,128]{4,3,2,1,0:T(4,128)} %pl_hbm.1), custom_call_target="tpu_custom_call" | custom-call | tf_op jit(solution)/shard_map/pallas_call | solution.py:626
  9.2 0.8 %shard_map.60 = (f32[2,256,128]{2,1,0:T(8,128)}, f32[2,2,64,128]{3,2,1,0:T(8,128)}) custom-call(f32[2,256,128]{2,1,0:T(8,128)S(1)} %get-tuple-element.6.f_ref, f32[2,2,64,128]{3,2,1,0:T(8,128)S(1)} %get-tuple-element.7.p_ref), custom_call_target="tpu_custom_call" | custom-call | tf_op jit(solution)/shard_map/pallas_call | solution.py:654

commit v4 on v3

--- a/solution.py
+++ b/solution.py
@@ -103,9 +103,9 @@
         return (target + along) + (across + z_part(v))
 
     def sides(k):
-        px = grid.x_closed(k + grid.xp(k))
-        py = grid.y_closed(k + grid.yp(k))
-        return px, grid.xm(px), py, grid.ym(py)
+        px, mx = grid.x_faces(k)
+        py, my = grid.y_faces(k)
+        return px, mx, py, my
 
     def coefficients(k):
         px, mx, py, my = sides(k)
@@ -129,6 +129,8 @@
         ions = ion_base * jnp.exp2((thermal_slope * log2_e) * old_t)
         target_t = old_t + heating[step] * (2.0 + old_n * old_n)
         ion_faces, ion_robin, ion_inv = coefficients(ions)
+        if step == 0:
+            yield
         return (
             (old_t, target_t, sweep(old_t, target_t, heat_faces), heat_faces, heat_robin, heat_inv),
             (old_n, old_n, sweep(old_n, old_n, ion_faces), ion_faces, ion_robin, ion_inv),
@@ -142,10 +144,12 @@
             out.append(sweep(first, target + given, faces) * (take_new * inv) - keep_old * old)
         return out
 
-    parts = open_step(0, old_t, old_n)
+    yield
+    parts = yield from open_step(0, old_t, old_n)
     trace = yield
     early = close_step(parts, 0, trace)
-    yield early, close_step(open_step(1, *early), 1, trace)
+    parts = yield from open_step(1, *early)
+    yield early, close_step(parts, 1, trace)
 
 
 class Rolled:
@@ -161,10 +165,14 @@
     def ym(self, v):
         return roll_last(v, 1)
 
-    def x_closed(self, face):
-        half = face[..., 8:, :]
-        rows = lax.broadcasted_iota(jnp.int32, (1,) * (face.ndim - 2) + (8, C), face.ndim - 2)
-        return jnp.concatenate([face[..., :8, :], jnp.where(rows == 7, 0.0, half)], axis=face.ndim - 2)
+    def x_faces(self, k):
+        rows = lax.broadcasted_iota(jnp.int32, (1,) * (k.ndim - 2) + (8, C), k.ndim - 2)
+        up, down = k + self.xp(k), k + self.xm(k)
+        axis = k.ndim - 2
+        return (
+            jnp.concatenate([up[..., :8, :], jnp.where(rows == 7, 0.0, up[..., 8:, :])], axis=axis),
+            jnp.concatenate([jnp.where(rows == 0, 0.0, down[..., :8, :]), down[..., 8:, :]], axis=axis),
+        )
 
 
 class Span:
@@ -221,11 +229,11 @@
 
     def ion_parts(self, temper, lo, hi):
         k = self.ion_base[lo:hi] * jnp.exp2((thermal_slope * log2_e) * temper(lo, hi))
-        py = k + roll_last(k, -1)
         row = lax.broadcasted_iota(jnp.int32, (1, 8, C), 1)
-        pz = k + roll_rows(k, -1)
+        pz, mz = k + roll_rows(k, -1), k + roll_rows(k, 1)
         pz = jnp.concatenate([pz[:, :8], jnp.where(row == 7, 0.0, pz[:, 8:])], axis=1)
-        return k, py, roll_last(py, 1), pz, roll_rows(pz, 1)
+        mz = jnp.concatenate([jnp.where(row == 0, 0.0, mz[:, :8]), mz[:, 8:]], axis=1)
+        return k, k + roll_last(k, -1), k + roll_last(k, 1), pz, mz
 
     def ion_spans(self, temper, lo, hi):
         parts = [self.ion_parts(temper, a, min(a + 4, hi)) for a in range(lo, hi, 4)]
@@ -308,6 +316,7 @@
             low = self.last(old[f], target, first, faces, inv, 0, 2)
             high = self.last(old[f], target, first, faces, inv, X - 2, X)
             news.append(joined(low, self.mid1[f], high))
+            yield
         low, high = self.ion_spans(news[0], 0, 2), self.ion_spans(news[0], X - 2, X)
         spans = [joined(a, b, c) for a, b, c in zip(low, self.spans1, high)]
         k = spans[0].values
@@ -315,6 +324,7 @@
             jnp.concatenate([k[1:3] + k[0:2], self.face1.values, k[X - 2 :] + k[X - 3 : X - 1]], axis=0), 0
         )
         inv = joined(self.ion_inverse(spans, face, 0, 3), self.inv1, self.ion_inverse(spans, face, X - 3, X))
+        yield
         low, high = self.targets(1, news, 0, 2), self.targets(1, news, X - 2, X)
         ends = []
         for f, (faces, inv, k) in enumerate((self.heat, ((face, *spans[1:]), inv, spans[0]))):
@@ -339,7 +349,8 @@
                     self.last(news[f], target, first, faces, inv, X - 4, X),
                 )
             )
-        return news, ends
+            yield
+        self.states = news, ends
 
 
 class Strips(Rolled):
@@ -350,12 +361,15 @@
         layer = 8 * lax.broadcasted_iota(jnp.int32, (1, 2, 1, 1), 1) + self.lane // 16
         side = lax.broadcasted_iota(jnp.int32, (2, 1, 1, 1), 0)
         self.edge4 = jnp.where((rows == 0) | (rows == X - 1), 4.0, 0.0)
-        self.between = jnp.where(self.column == 7, jnp.where(side == 0, left_open, right_open), 1.0)
+        opened = jnp.where(side == 0, left_open, right_open)
+        self.between_up = jnp.where(self.column == 7, opened, 1.0)
+        self.between_down = jnp.where(self.column == 8, opened, 1.0)
         self.below_top = (layer < Z - 1).astype(jnp.float32)
+        self.above_floor = (layer > 0).astype(jnp.float32)
         self.decay = jnp.exp(-4.0 * layer.astype(jnp.float32) / Z)
 
-    def y_closed(self, face):
-        return face * self.between
+    def y_faces(self, k):
+        return (k + self.yp(k)) * self.between_up, (k + self.ym(k)) * self.between_down
 
     def zp(self, v):
         moved = roll_last(v, -16)
@@ -367,12 +381,12 @@
 
     def layers(self, k):
         up = (k + self.zp(k)) * self.below_top
-        down = self.zm(up)
+        down = (k + self.zm(k)) * self.above_floor
         return lambda v: up * self.zp(v) + down * self.zm(v), up + down
 
     def even_layers(self, k, diagonal):
-        up = jnp.broadcast_to(2.0 * k, k.shape[:1] + (2,) + k.shape[2:]) * self.below_top
-        down = self.zm(up)
+        twice = jnp.broadcast_to(2.0 * k, k.shape[:1] + (2,) + k.shape[2:])
+        up, down = twice * self.below_top, twice * self.above_floor
         return lambda v: up * self.zp(v) + down * self.zm(v), inverse(diagonal + (up + down))
 
 
@@ -529,13 +543,8 @@
         row = (step * 2 + field) * Z
         return recv_g[side, row : row + Z, :][None]
 
-    early, late = columns.after(trace_own)
-    for f in range(2):
-        for x in range(X):
-            of_ref[f, pl.ds(x, Z, stride=X), :] = late[f].values[x]
-        for p, x in enumerate((0, 1, X - 2, X - 1)):
-            op_ref[0, f, pl.ds(p, Z, stride=4), :] = early[f].values[x]
-
+    rest = columns.after(trace_own)
+    next(rest)
     grid = Strips((gy > 0).astype(jnp.float32), (gy < n_gy - 1).astype(jnp.float32))
     inner = grid.column < 8
 
@@ -554,6 +563,7 @@
             halves.append(jnp.broadcast_to(both, (2, 2, 8, C)))
         return jnp.concatenate(halves, axis=2)
 
+    next(rest)
     fields = [strip([wider(recv_b[i, f]) for i in range(2)], own_b[2 * f : 2 * f + 2]) for f in range(2)]
     drop = strip([recv_b[0, 0], recv_b[1, 0]], own_b[4])
     on0 = strip([roll_last(recv_b[0, 1], 1), roll_last(recv_b[1, 1], -1)], own_b[5])
@@ -566,7 +576,14 @@
         grid.decay,
         grid,
     )
-    next(work)
+    for _ in rest:
+        next(work)
+    early, late = columns.states
+    for f in range(2):
+        for x in range(X):
+            of_ref[f, pl.ds(x, Z, stride=X), :] = late[f].values[x]
+        for p, x in enumerate((0, 1, X - 2, X - 1)):
+            op_ref[0, f, pl.ds(p, Z, stride=4), :] = early[f].values[x]
     for offset in CORNERS:
         wait_from(offset)
     strips = work.send(trace_strip)

time: 10.1 us -> 9.84 us (0.974)
  Pallas kernels: 9.32 us -> 9.07 us
    pallas_call x1, Pallas kernels: 8.56 us -> 8.31 us  [shards(): pl.pallas_call(functools.partial(kernel, n_gx, n_gy), out_shape=(jax.Shap...]
where the time goes in v4:
time: 9.84 us; the launch traced here: 9.71 us
  Pallas kernels  9.07 us (92%)
  between operations  0.64 us (7%)
    pallas_call x1, Pallas kernels, shards(): pl.pallas_call(functools.partial(kernel, n_gx, n_gy), out_shape=(jax.Shap...  8.31 us
    pallas_call x1, Pallas kernels, shards(): pl.pallas_call(write_out, out_shape=(pltpu.HBM((2, Z * X, C), jnp.float32...  0.76 us

profile of v4, /device:TPU:57, one launch (start us, length us, event | category | flops | bytes accessed | tf_op | source)
XLA Modules:
  0.0 9.7 jit_solution(17221018393921415245)
XLA Ops:
  0.6 8.3 %shard_map.59 = (f32[2,256,128]{2,1,0:T(8,128)S(1)}, f32[2,2,64,128]{3,2,1,0:T(8,128)S(1)}) custom-call(bf16[2,16,16,128]{3,2,1,0:T(8,128)(2,1)} %f_hbm.1, s32[16,128]{1,0:T(8,128)} %ph_hbm.1, s32[2,16,128]{2,1,0:T(8,128)} %el_hbm.1, f32[2,2,16,4,128]{4,3,2,1,0:T(4,128)} %pl_hbm.1), custom_call_target="tpu_custom_call" | custom-call | tf_op jit(solution)/shard_map/pallas_call | solution.py:643
  8.9 0.8 %shard_map.60 = (f32[2,256,128]{2,1,0:T(8,128)}, f32[2,2,64,128]{3,2,1,0:T(8,128)}) custom-call(f32[2,256,128]{2,1,0:T(8,128)S(1)} %get-tuple-element.6.f_ref, f32[2,2,64,128]{3,2,1,0:T(8,128)S(1)} %get-tuple-element.7.p_ref), custom_call_target="tpu_custom_call" | custom-call | tf_op jit(solution)/shard_map/pallas_call | solution.py:671

commit v5 on v4

--- a/solution.py
+++ b/solution.py
@@ -24,6 +24,7 @@
 Z = 16
 X = 16
 C = 128
+PITCH = 17
 CORNERS = ((-1, -1), (-1, 1), (1, -1), (1, 1))
 SIDES_Y = ((0, -1), (0, 1))
 SIDES_X = ((-1, 0), (1, 0))
@@ -39,22 +40,39 @@
 
 
 def roll_rows(v, shift):
-    return pltpu.roll(v, shift % X, v.ndim - 2)
-
-
-def row_masks(ndim):
-    shape = (1,) * (ndim - 2) + (X, C)
-    rows = lax.broadcasted_iota(jnp.int32, shape, ndim - 2)
-    return rows
+    return pltpu.roll(v, shift % 8, v.ndim - 2)
+
+
+def rows_of(ref, index, start, step):
+    at = lambda first: ref[(*index, pl.ds(first, 8, stride=step), slice(None))]
+    return jnp.stack([at(start), at(start + step // 2)], axis=0)
+
+
+def next_of(v, axis, turn):
+    even, odd = lax.slice_in_dim(v, 0, 1, axis=axis), lax.slice_in_dim(v, 1, 2, axis=axis)
+    return jnp.concatenate([odd, turn(even)], axis=axis)
+
+
+def previous_of(v, axis, turn):
+    even, odd = lax.slice_in_dim(v, 0, 1, axis=axis), lax.slice_in_dim(v, 1, 2, axis=axis)
+    return jnp.concatenate([turn(odd), even], axis=axis)
+
+
+def faces_of(k, axis, forth, back, last, first):
+    even, odd = lax.slice_in_dim(k, 0, 1, axis=axis), lax.slice_in_dim(k, 1, 2, axis=axis)
+    inner = even + odd
+    up = jnp.where(last, 0.0, odd + forth(even))
+    down = jnp.where(first, 0.0, even + back(odd))
+    return jnp.concatenate([inner, up], axis=axis), jnp.concatenate([down, inner], axis=axis)
 
 
 def packed_columns(v):
     head = v.shape[:-3]
-    v = v.reshape(head + (2, 8, X, C))
+    v = v.reshape(head + (8, 2, X, C))
     lane = lanes(head + (2, X, C))
     out = None
     for j in range(8):
-        moved = roll_last(v[..., j, :, :], 16 * j + 8)
+        moved = roll_last(v[..., j, :, :, :], 16 * j + 8)
         out = moved if out is None else jnp.where(lane >= 16 * j, moved, out)
     return out
 
@@ -82,14 +100,6 @@
     return out
 
 
-def wider(v):
-    v = jnp.stack([roll_last(v, 4), roll_last(v, -60)], axis=v.ndim - 2)
-    lane = lanes(v.shape)
-    v = jnp.where(lane >= 64, roll_last(v, 32), v)
-    v = jnp.where(lane % 64 >= 32, roll_last(v, 16), v)
-    return jnp.where(lane % 32 >= 16, roll_last(v, 8), v)
-
-
 def inverse(v):
     guess = pl.reciprocal(v, approx=True)
     return guess * (2.0 - v * guess)
@@ -103,9 +113,7 @@
         return (target + along) + (across + z_part(v))
 
     def sides(k):
-        px, mx = grid.x_faces(k)
-        py, my = grid.y_faces(k)
-        return px, mx, py, my
+        return (*grid.x_faces(k), *grid.y_faces(k))
 
     def coefficients(k):
         px, mx, py, my = sides(k)
@@ -150,29 +158,6 @@
     early = close_step(parts, 0, trace)
     parts = yield from open_step(1, *early)
     yield early, close_step(parts, 1, trace)
-
-
-class Rolled:
-    def xp(self, v):
-        return roll_rows(v, -1)
-
-    def xm(self, v):
-        return roll_rows(v, 1)
-
-    def yp(self, v):
-        return roll_last(v, -1)
-
-    def ym(self, v):
-        return roll_last(v, 1)
-
-    def x_faces(self, k):
-        rows = lax.broadcasted_iota(jnp.int32, (1,) * (k.ndim - 2) + (8, C), k.ndim - 2)
-        up, down = k + self.xp(k), k + self.xm(k)
-        axis = k.ndim - 2
-        return (
-            jnp.concatenate([up[..., :8, :], jnp.where(rows == 7, 0.0, up[..., 8:, :])], axis=axis),
-            jnp.concatenate([jnp.where(rows == 0, 0.0, down[..., :8, :]), down[..., 8:, :]], axis=axis),
-        )
 
 
 class Span:
@@ -219,20 +204,17 @@
         my = roll_last(py, 1)
         edge = jnp.concatenate([heat[:1], jnp.zeros_like(heat[1:-1]), heat[-1:]], axis=0)
         base = (1.0 + 4.0 * edge) + x_sum(face, None, 0, X) + (py + my)
-        twice = both(2.0 * heat)
-        row = lax.broadcasted_iota(jnp.int32, (1, Z, C), 1)
-        pz = jnp.where(row == Z - 1, 0.0, twice)
-        mz = jnp.where(row == 0, 0.0, twice)
+        row = lax.broadcasted_iota(jnp.int32, (1, 1, 8, 1), 2)
+        self.high, self.low = row == 7, row == 0
+        pz = jnp.concatenate([2.0 * heat, jnp.where(self.high, 0.0, 2.0 * heat)], axis=1)
+        mz = jnp.concatenate([jnp.where(self.low, 0.0, 2.0 * heat), 2.0 * heat], axis=1)
         heat_faces = (Span(both(face.values), 0), Span(both(py), 0), Span(both(my), 0), Span(pz, 0), Span(mz, 0))
         self.heat = (heat_faces, Span(inverse(both(base) + (pz + mz)), 0), Span(both(heat), 0))
         self.states = []
 
     def ion_parts(self, temper, lo, hi):
         k = self.ion_base[lo:hi] * jnp.exp2((thermal_slope * log2_e) * temper(lo, hi))
-        row = lax.broadcasted_iota(jnp.int32, (1, 8, C), 1)
-        pz, mz = k + roll_rows(k, -1), k + roll_rows(k, 1)
-        pz = jnp.concatenate([pz[:, :8], jnp.where(row == 7, 0.0, pz[:, 8:])], axis=1)
-        mz = jnp.concatenate([jnp.where(row == 0, 0.0, mz[:, :8]), mz[:, 8:]], axis=1)
+        pz, mz = faces_of(k, 1, lambda u: roll_rows(u, -1), lambda u: roll_rows(u, 1), self.high, self.low)
         return k, k + roll_last(k, -1), k + roll_last(k, 1), pz, mz
 
     def ion_spans(self, temper, lo, hi):
@@ -255,7 +237,9 @@
         face, py, my, pz, mz = faces
         mid = v(a, b)
         across = py(a, b) * roll_last(mid, -1) + my(a, b) * roll_last(mid, 1)
-        upright = pz(a, b) * roll_rows(mid, -1) + mz(a, b) * roll_rows(mid, 1)
+        above = next_of(mid, 1, lambda u: roll_rows(u, -1))
+        below = previous_of(mid, 1, lambda u: roll_rows(u, 1))
+        upright = pz(a, b) * above + mz(a, b) * below
         return (target(a, b) + x_sum(face, v, a, b)) + (across + upright)
 
     def targets(self, step, old, lo, hi):
@@ -353,40 +337,54 @@
         self.states = news, ends
 
 
-class Strips(Rolled):
+class Strips:
     def __init__(self, left_open, right_open):
-        rows = row_masks(4)
-        self.lane = lanes((1, 1, 1, C))
+        self.lane = lanes((1, 1, 1, 1, C))
         self.column = self.lane % 16
-        layer = 8 * lax.broadcasted_iota(jnp.int32, (1, 2, 1, 1), 1) + self.lane // 16
-        side = lax.broadcasted_iota(jnp.int32, (2, 1, 1, 1), 0)
-        self.edge4 = jnp.where((rows == 0) | (rows == X - 1), 4.0, 0.0)
+        row = lax.broadcasted_iota(jnp.int32, (1, 1, 1, 8, 1), 3)
+        half_x = lax.broadcasted_iota(jnp.int32, (1, 1, 2, 1, 1), 2)
+        half_z = lax.broadcasted_iota(jnp.int32, (1, 2, 1, 1, 1), 1)
+        side = lax.broadcasted_iota(jnp.int32, (2, 1, 1, 1, 1), 0)
+        self.low, self.high = row == 0, row == 7
+        self.floor, self.top = self.lane < 16, self.lane >= 112
+        self.edge4 = jnp.where(2 * row + half_x == 0, 4.0, 0.0) + jnp.where(2 * row + half_x == X - 1, 4.0, 0.0)
         opened = jnp.where(side == 0, left_open, right_open)
         self.between_up = jnp.where(self.column == 7, opened, 1.0)
         self.between_down = jnp.where(self.column == 8, opened, 1.0)
-        self.below_top = (layer < Z - 1).astype(jnp.float32)
-        self.above_floor = (layer > 0).astype(jnp.float32)
-        self.decay = jnp.exp(-4.0 * layer.astype(jnp.float32) / Z)
+        self.decay = jnp.exp(-4.0 * (2 * (self.lane // 16) + half_z).astype(jnp.float32) / Z)
+
+    def xp(self, v):
+        return next_of(v, 2, lambda u: roll_rows(u, -1))
+
+    def xm(self, v):
+        return previous_of(v, 2, lambda u: roll_rows(u, 1))
+
+    def yp(self, v):
+        return roll_last(v, -1)
+
+    def ym(self, v):
+        return roll_last(v, 1)
+
+    def zp(self, v):
+        return next_of(v, 1, lambda u: roll_last(u, -16))
+
+    def zm(self, v):
+        return previous_of(v, 1, lambda u: roll_last(u, 16))
+
+    def x_faces(self, k):
+        return faces_of(k, 2, lambda u: roll_rows(u, -1), lambda u: roll_rows(u, 1), self.high, self.low)
 
     def y_faces(self, k):
         return (k + self.yp(k)) * self.between_up, (k + self.ym(k)) * self.between_down
 
-    def zp(self, v):
-        moved = roll_last(v, -16)
-        return jnp.where(self.lane < 112, moved, jnp.concatenate([moved[:, 1:2], moved[:, 0:1]], axis=1))
-
-    def zm(self, v):
-        moved = roll_last(v, 16)
-        return jnp.where(self.lane >= 16, moved, jnp.concatenate([moved[:, 1:2], moved[:, 0:1]], axis=1))
-
     def layers(self, k):
-        up = (k + self.zp(k)) * self.below_top
-        down = (k + self.zm(k)) * self.above_floor
+        up, down = faces_of(k, 1, lambda u: roll_last(u, -16), lambda u: roll_last(u, 16), self.top, self.floor)
         return lambda v: up * self.zp(v) + down * self.zm(v), up + down
 
     def even_layers(self, k, diagonal):
-        twice = jnp.broadcast_to(2.0 * k, k.shape[:1] + (2,) + k.shape[2:])
-        up, down = twice * self.below_top, twice * self.above_floor
+        twice = 2.0 * k
+        up = jnp.concatenate([twice, jnp.where(self.top, 0.0, twice)], axis=1)
+        down = jnp.concatenate([jnp.where(self.floor, 0.0, twice), twice], axis=1)
         return lambda v: up * self.zp(v) + down * self.zm(v), inverse(diagonal + (up + down))
 
 
@@ -410,6 +408,8 @@
     recv_b,
     recv_g,
     recv_c,
+    merge_ref,
+    late_ref,
     in_sem,
     send_sem,
     recv_sem,
@@ -474,20 +474,22 @@
     send_b[0, 1] = jnp.where(place >= 4, near[1], jnp.where(place == 0, roll_last(on1, -4), roll_last(on0, -3)))
     send_b[1, 0] = jnp.where(place < 4, near[0], roll_last(drop, 4))
     send_b[1, 1] = jnp.where(place < 4, near[1], jnp.where(place == 7, roll_last(on1, 4), roll_last(on0, 3)))
-    own_row = lax.broadcasted_iota(jnp.int32, (Z, C), 0) % 8 == lanes((Z, C)) // 16
+    own_row = lax.broadcasted_iota(jnp.int32, (8, C), 0) == lanes((8, C)) // 16
     for side in range(2):
         near, far = ((0, 1), (3, 2))[side]
         for s in range(2):
             for f in range(2):
-                a = pl_in[s, f, :, near, :]
-                b = pl_in[s, f, :, far, :]
-                g = a + 0.5 * (a - b)
-                row = (s * 2 + f) * Z
-                send_g[side, row : row + Z, :] = g
-                spread = pltpu.roll(g, 8, 1, stride=16, stride_axis=0)
-                spread = jnp.where(own_row, spread, 0.0).reshape(2, 8, C)
-                row = 64 + (s * 2 + f) * 2
-                send_g[side, row : row + 2, :] = jnp.sum(spread, axis=1)
+                first = (s * 2 + f) * Z
+                a = pl_in[pl.ds(4 * first + near, Z, stride=4), :]
+                b = pl_in[pl.ds(4 * first + far, Z, stride=4), :]
+                send_g[side, first : first + Z, :] = a + 0.5 * (a - b)
+    for side in range(2):
+        for row in range(4):
+            halves = rows_of(send_g, (side,), row * Z, 2)
+            for h in range(2):
+                spread = pltpu.roll(halves[h], 8, 1, stride=16, stride_axis=0)
+                spread = jnp.sum(jnp.where(own_row, spread, 0.0), axis=0, keepdims=True)
+                send_g[side, 64 + 2 * row + h : 65 + 2 * row + h, :] = spread
 
     pl.semaphore_wait(barrier, expected)
 
@@ -529,10 +531,13 @@
             copy_of(ALL.index(back), back).wait_recv()
 
     for f in range(2):
-        f_32[f] = f_in[f].astype(jnp.float32).reshape(Z * X, C)
-    planes_x = lambda f: jnp.stack([f_32[f, pl.ds(x, Z, stride=X), :] for x in range(X)], axis=0)
-    rows = lambda v: jnp.broadcast_to(v[:, None, :], (X, 8, C))
-    height = lax.broadcasted_iota(jnp.int32, (1, Z, C), 1)
+        layers = f_in[f].astype(jnp.float32)
+        for z in range(Z):
+            f_32[f, PITCH * z : PITCH * z + X, :] = layers[z]
+    planes_x = lambda f: jnp.stack([rows_of(f_32, (f,), x, 2 * PITCH) for x in range(X)], axis=0)
+    rows = lambda v: jnp.broadcast_to(v[:, None, None, :], (X, 1, 8, C))
+    half = lax.broadcasted_iota(jnp.int32, (1, 2, 1, 1), 1)
+    height = 2 * lax.broadcasted_iota(jnp.int32, (1, 1, 8, C), 2) + half
     decay = jnp.exp(-4.0 * height.astype(jnp.float32) / Z)
     columns = OwnColumns(rows(maps[0]), [rows(maps[1]), rows(maps[2])], planes_x(0), planes_x(1), decay)
     columns.before()
@@ -540,17 +545,26 @@
         wait_from(offset)
 
     def trace_own(step, field, side):
-        row = (step * 2 + field) * Z
-        return recv_g[side, row : row + Z, :][None]
+        return rows_of(recv_g, (side,), (step * 2 + field) * Z, 2)[None]
 
     rest = columns.after(trace_own)
     next(rest)
     grid = Strips((gy > 0).astype(jnp.float32), (gy < n_gy - 1).astype(jnp.float32))
-    inner = grid.column < 8
+    inner = grid.column[0] < 8
 
     def strip(outer, own):
-        inside = inner[0, 0]
-        return jnp.stack([jnp.where(inside, outer[0], own), jnp.where(inside, own, outer[1])], axis=0)
+        return jnp.stack([jnp.where(inner, outer[0], own), jnp.where(inner, own, outer[1])], axis=0)
+
+    def halo(side, field):
+        v = rows_of(recv_b, (side, field), 0, 2)
+        return jnp.stack([roll_last(v, 4), roll_last(v, -4)], axis=0)
+
+    def own_strip(i):
+        return rows_of(own_b, (i,), 0, 2)
+
+    def map_strip(field, own, turns):
+        outer = [roll_last(rows_of(recv_b, (side, field), 0, 2), turns[side])[None] for side in range(2)]
+        return strip(outer, own_strip(own)[None])
 
     def trace_strip(step, field):
         row = (step * 2 + field) * 2
@@ -559,18 +573,20 @@
             mid = recv_g[i, 64 + row : 66 + row, :]
             low = jnp.where(inner[0, 0], recv_c[2 * i, row : row + 2, :], mid)
             high = jnp.where(inner[0, 0], mid, recv_c[2 * i + 1, row : row + 2, :])
-            both = jnp.stack([low, high], axis=0)[:, :, None, :]
-            halves.append(jnp.broadcast_to(both, (2, 2, 8, C)))
-        return jnp.concatenate(halves, axis=2)
+            halves.append(jnp.broadcast_to(jnp.stack([low, high], axis=0)[:, :, None, :], (2, 2, 8, C)))
+        return jnp.stack(halves, axis=2)
 
     next(rest)
-    fields = [strip([wider(recv_b[i, f]) for i in range(2)], own_b[2 * f : 2 * f + 2]) for f in range(2)]
-    drop = strip([recv_b[0, 0], recv_b[1, 0]], own_b[4])
-    on0 = strip([roll_last(recv_b[0, 1], 1), roll_last(recv_b[1, 1], -1)], own_b[5])
-    on1 = strip([recv_b[0, 1], recv_b[1, 1]], own_b[6])
+    fields = [
+        strip([halo(side, f) for side in range(2)], jnp.stack([own_strip(2 * f), own_strip(2 * f + 1)], axis=0))
+        for f in range(2)
+    ]
+    drop = map_strip(0, 4, (0, 0))
+    on0 = map_strip(1, 5, (1, -1))
+    on1 = map_strip(1, 6, (0, 0))
     work = steps_of(
-        drop[:, None],
-        [on0[:, None], on1[:, None]],
+        drop,
+        [on0, on1],
         fields[0],
         fields[1],
         grid.decay,
@@ -580,40 +596,45 @@
         next(work)
     early, late = columns.states
     for f in range(2):
-        for x in range(X):
-            of_ref[f, pl.ds(x, Z, stride=X), :] = late[f].values[x]
-        for p, x in enumerate((0, 1, X - 2, X - 1)):
-            op_ref[0, f, pl.ds(p, Z, stride=4), :] = early[f].values[x]
+        for h in range(2):
+            for x in range(X):
+                late_ref[f, pl.ds(PITCH * x + h, 8, stride=2), :] = late[f].values[x, h]
+            for p, x in enumerate((0, 1, X - 2, X - 1)):
+                op_ref[0, f, pl.ds(p + 4 * h, 8, stride=8), :] = early[f].values[x, h]
     for offset in CORNERS:
         wait_from(offset)
     strips = work.send(trace_strip)
     lane = lanes((X, C))
     edge = (lane < 4) | (lane >= C - 4)
 
-    def four(v):
-        return [v[..., 0:2, :], v[..., X - 2 : X, :]]
-
     def both_sides(state):
-        return jnp.where(inner[0], state[1], state[0])
-
-    early = jnp.concatenate(four(both_sides(strips[0][0])) + four(both_sides(strips[0][1])), axis=1)
+        return jnp.where(inner, state[1], state[0])
+
+    four = []
+    for f in range(2):
+        state = both_sides(strips[0][f])
+        four += [state[:, 0, 0:1], state[:, 1, 0:1], state[:, 0, 7:8], state[:, 1, 7:8]]
+    four = jnp.concatenate(four, axis=1)
     for j in range(8):
-        back = roll_last(early, -(16 * j + 8))
+        back = roll_last(four, -(16 * j + 8))
         for h in range(2):
-            z = 8 * h + j
             for f in range(2):
-                rows = slice(4 * z, 4 * z + 4)
+                rows = slice(4 * (2 * j + h), 4 * (2 * j + h) + 4)
                 op_ref[0, f, rows, :] = jnp.where(edge[:4], back[h, 4 * f : 4 * f + 4], op_ref[0, f, rows, :])
     for f in range(2):
-        merged = both_sides(strips[1][f])
-        for j in range(8):
-            back = roll_last(merged, -(16 * j + 8))
-            for h in range(2):
-                z = 8 * h + j
+        state = both_sides(strips[1][f])
+        for h in range(2):
+            for i in range(2):
+                merge_ref[f, h, pl.ds(i, 8, stride=2), :] = state[h, i]
+    for f in range(2):
+        for h in range(2):
+            state = merge_ref[f, h]
+            for j in range(8):
+                z = 2 * j + h
                 rows = slice(X * z, X * z + X)
-                value = jnp.where(edge, back[h], of_ref[f, rows, :])
+                value = jnp.where(edge, roll_last(state, -(16 * j + 8)), late_ref[f, pl.ds(z, X, stride=PITCH), :])
                 of_ref[f, rows, :] = value
-                op_ref[1, f, 4 * z : 4 * z + 4, :] = jnp.concatenate(four(value), axis=0)
+                op_ref[1, f, 4 * z : 4 * z + 4, :] = jnp.concatenate([value[0:2], value[X - 2 :]], axis=0)
 
     for i, offset in enumerate(ALL):
 
@@ -650,16 +671,18 @@
             out_specs=(vmem, vmem),
             scratch_shapes=[
                 pltpu.VMEM((2, Z, X, C), jnp.bfloat16),
-                pltpu.VMEM((2, Z * X, C), jnp.float32),
+                pltpu.VMEM((2, Z * PITCH, C), jnp.float32),
                 pltpu.VMEM((X, C), jnp.int32),
                 pltpu.VMEM((2, X, C), jnp.int32),
-                pltpu.VMEM((2, 2, Z, 4, C), jnp.float32),
+                pltpu.VMEM((2 * 2 * Z * 4, C), jnp.float32),
                 pltpu.VMEM((7, X, C), jnp.float32),
                 pltpu.VMEM((2, 2, X, C), jnp.float32),
                 pltpu.VMEM((2, 72, C), jnp.float32),
                 pltpu.VMEM((2, 2, X, C), jnp.float32),
                 pltpu.VMEM((2, 72, C), jnp.float32),
                 pltpu.VMEM((4, 8, C), jnp.float32),
+                pltpu.VMEM((2, 2, X, C), jnp.float32),
+                pltpu.VMEM((2, PITCH * X, C), jnp.float32),
                 pltpu.SemaphoreType.DMA((4,)),
                 pltpu.SemaphoreType.DMA((8,)),
                 pltpu.SemaphoreType.DMA((8,)),
@@ -667,7 +690,7 @@
             compiler_params=pltpu.CompilerParams(
                 collective_id=0, has_side_effects=True, vmem_limit_bytes=32 * 1024 * 1024
             ),
-        )(*[pltpu.with_memory_space_constraint(v, pltpu.HBM) for v in (fields, phase, electrode, planes)])
+        )(*[pltpu.with_memory_space_constraint(v, pltpu.HBM) for v in (fields, phase, electrode, planes.reshape(2 * 2 * Z * 4, C))])
         new_fields, new_planes = pl.pallas_call(
             write_out,
             out_shape=(

time: 9.84 us -> 9.66 us (0.982)
  Pallas kernels: 9.07 us -> 8.89 us
    pallas_call x1, Pallas kernels: 8.31 us -> 8.13 us  [shards(): pl.pallas_call(functools.partial(kernel, n_gx, n_gy), out_shape=(jax.Shap...]
where the time goes in v5:
time: 9.66 us; the launch traced here: 9.53 us
  Pallas kernels  8.89 us (92%)
  between operations  0.64 us (7%)
    pallas_call x1, Pallas kernels, shards(): pl.pallas_call(functools.partial(kernel, n_gx, n_gy), out_shape=(jax.Shap...  8.13 us
    pallas_call x1, Pallas kernels, shards(): pl.pallas_call(write_out, out_shape=(pltpu.HBM((2, Z * X, C), jnp.float32...  0.76 us

profile of v5, /device:TPU:57, one launch (start us, length us, event | category | flops | bytes accessed | tf_op | source)
XLA Modules:
  0.0 9.5 jit_solution(1153893782824855332)
XLA Ops:
  0.6 8.1 %shard_map.59 = (f32[2,256,128]{2,1,0:T(8,128)S(1)}, f32[2,2,64,128]{3,2,1,0:T(8,128)S(1)}) custom-call(bf16[2,16,16,128]{3,2,1,0:T(8,128)(2,1)} %f_hbm.1, s32[16,128]{1,0:T(8,128)} %ph_hbm.1, s32[2,16,128]{2,1,0:T(8,128)} %el_hbm.1, f32[256,128]{1,0:T(8,128)} %bitcast.3), custom_call_target="tpu_custom_call" | custom-call | tf_op jit(solution)/shard_map/pallas_call | solution.py:664
  8.8 0.8 %shard_map.60 = (f32[2,256,128]{2,1,0:T(8,128)}, f32[2,2,64,128]{3,2,1,0:T(8,128)}) custom-call(f32[2,256,128]{2,1,0:T(8,128)S(1)} %get-tuple-element.6.f_ref, f32[2,2,64,128]{3,2,1,0:T(8,128)S(1)} %get-tuple-element.7.p_ref), custom_call_target="tpu_custom_call" | custom-call | tf_op jit(solution)/shard_map/pallas_call | solution.py:694

commit v6 on v5

--- a/solution.py
+++ b/solution.py
@@ -144,20 +144,20 @@
             (old_n, old_n, sweep(old_n, old_n, ion_faces), ion_faces, ion_robin, ion_inv),
         )
 
-    def close_step(parts, step, trace):
-        out = []
-        for field, (old, target, total, faces, robin, inv) in enumerate(parts):
-            given = robin * trace(step, field)
-            first = (total + given) * inv
-            out.append(sweep(first, target + given, faces) * (take_new * inv) - keep_old * old)
-        return out
+    def close_field(parts, step, field, trace):
+        old, target, total, faces, robin, inv = parts[field]
+        given = robin * trace(step, field)
+        first = (total + given) * inv
+        return sweep(first, target + given, faces) * (take_new * inv) - keep_old * old
 
     yield
     parts = yield from open_step(0, old_t, old_n)
     trace = yield
-    early = close_step(parts, 0, trace)
+    early = [close_field(parts, 0, field, trace) for field in range(2)]
+    yield early
     parts = yield from open_step(1, *early)
-    yield early, close_step(parts, 1, trace)
+    for field in range(2):
+        yield close_field(parts, 1, field, trace)
 
 
 class Span:
@@ -410,7 +410,6 @@
     recv_c,
     merge_ref,
     late_ref,
-    in_sem,
     send_sem,
     recv_sem,
 ):
@@ -440,7 +439,7 @@
         expected = expected + exists(offset).astype(jnp.int32)
 
     loads = [
-        pltpu.make_async_copy(src, dst, in_sem.at[i])
+        pltpu.make_async_copy(src, dst, send_sem.at[i])
         for i, (src, dst) in enumerate(((ph_hbm, ph_in), (el_hbm, el_in), (f_hbm, f_in), (pl_hbm, pl_in)))
     ]
     for load in loads:
@@ -601,46 +600,49 @@
                 late_ref[f, pl.ds(PITCH * x + h, 8, stride=2), :] = late[f].values[x, h]
             for p, x in enumerate((0, 1, X - 2, X - 1)):
                 op_ref[0, f, pl.ds(p + 4 * h, 8, stride=8), :] = early[f].values[x, h]
+    for i, offset in enumerate(ALL):
+
+        @pl.when(exists(offset))
+        def _(i=i, offset=offset):
+            copy_of(i, offset).wait_send()
+
     for offset in CORNERS:
         wait_from(offset)
-    strips = work.send(trace_strip)
     lane = lanes((X, C))
     edge = (lane < 4) | (lane >= C - 4)
 
     def both_sides(state):
         return jnp.where(inner, state[1], state[0])
 
+    def merge(field, state):
+        state = both_sides(state)
+        for h in range(2):
+            for i in range(2):
+                merge_ref[field, h, pl.ds(i, 8, stride=2), :] = state[h, i]
+        for h in range(2):
+            state = merge_ref[field, h]
+            for j in range(8):
+                z = 2 * j + h
+                rows = slice(X * z, X * z + X)
+                own = late_ref[field, pl.ds(z, X, stride=PITCH), :]
+                value = jnp.where(edge, roll_last(state, -(16 * j + 8)), own)
+                of_ref[field, rows, :] = value
+                op_ref[1, field, 4 * z : 4 * z + 4, :] = jnp.concatenate([value[0:2], value[X - 2 :]], axis=0)
+
     four = []
-    for f in range(2):
-        state = both_sides(strips[0][f])
+    for state in work.send(trace_strip):
+        state = both_sides(state)
         four += [state[:, 0, 0:1], state[:, 1, 0:1], state[:, 0, 7:8], state[:, 1, 7:8]]
     four = jnp.concatenate(four, axis=1)
+    temper = next(work)
     for j in range(8):
         back = roll_last(four, -(16 * j + 8))
         for h in range(2):
             for f in range(2):
                 rows = slice(4 * (2 * j + h), 4 * (2 * j + h) + 4)
                 op_ref[0, f, rows, :] = jnp.where(edge[:4], back[h, 4 * f : 4 * f + 4], op_ref[0, f, rows, :])
-    for f in range(2):
-        state = both_sides(strips[1][f])
-        for h in range(2):
-            for i in range(2):
-                merge_ref[f, h, pl.ds(i, 8, stride=2), :] = state[h, i]
-    for f in range(2):
-        for h in range(2):
-            state = merge_ref[f, h]
-            for j in range(8):
-                z = 2 * j + h
-                rows = slice(X * z, X * z + X)
-                value = jnp.where(edge, roll_last(state, -(16 * j + 8)), late_ref[f, pl.ds(z, X, stride=PITCH), :])
-                of_ref[f, rows, :] = value
-                op_ref[1, f, 4 * z : 4 * z + 4, :] = jnp.concatenate([value[0:2], value[X - 2 :]], axis=0)
-
-    for i, offset in enumerate(ALL):
-
-        @pl.when(exists(offset))
-        def _(i=i, offset=offset):
-            copy_of(i, offset).wait_send()
+    merge(0, temper)
+    merge(1, next(work))
 
 
 def write_out(f_ref, p_ref, of_hbm, op_hbm, sem):
@@ -683,7 +685,6 @@
                 pltpu.VMEM((4, 8, C), jnp.float32),
                 pltpu.VMEM((2, 2, X, C), jnp.float32),
                 pltpu.VMEM((2, PITCH * X, C), jnp.float32),
-                pltpu.SemaphoreType.DMA((4,)),
                 pltpu.SemaphoreType.DMA((8,)),
                 pltpu.SemaphoreType.DMA((8,)),
             ],

time: 9.66 us -> 9.63 us (level)
  no operation moved by 1% of the time
where the time goes in v6:
time: 9.63 us; the launch traced here: 9.5 us
  Pallas kernels  8.86 us (92%)
  between operations  0.64 us (7%)
    pallas_call x1, Pallas kernels, shards(): pl.pallas_call(functools.partial(kernel, n_gx, n_gy), out_shape=(jax.Shap...  8.1 us
    pallas_call x1, Pallas kernels, shards(): pl.pallas_call(write_out, out_shape=(pltpu.HBM((2, Z * X, C), jnp.float32...  0.76 us

profile of v6, /device:TPU:57, one launch (start us, length us, event | category | flops | bytes accessed | tf_op | source)
XLA Modules:
  0.0 9.5 jit_solution(1238094933961239548)
XLA Ops:
  0.6 8.1 %shard_map.59 = (f32[2,256,128]{2,1,0:T(8,128)S(1)}, f32[2,2,64,128]{3,2,1,0:T(8,128)S(1)}) custom-call(bf16[2,16,16,128]{3,2,1,0:T(8,128)(2,1)} %f_hbm.1, s32[16,128]{1,0:T(8,128)} %ph_hbm.1, s32[2,16,128]{2,1,0:T(8,128)} %el_hbm.1, f32[256,128]{1,0:T(8,128)} %bitcast.3), custom_call_target="tpu_custom_call" | custom-call | tf_op jit(solution)/shard_map/pallas_call | solution.py:666
  8.7 0.8 %shard_map.60 = (f32[2,256,128]{2,1,0:T(8,128)}, f32[2,2,64,128]{3,2,1,0:T(8,128)}) custom-call(f32[2,256,128]{2,1,0:T(8,128)S(1)} %get-tuple-element.6.f_ref, f32[2,2,64,128]{3,2,1,0:T(8,128)S(1)} %get-tuple-element.7.p_ref), custom_call_target="tpu_custom_call" | custom-call | tf_op jit(solution)/shard_map/pallas_call | solution.py:695

commit v7 on v6

--- a/solution.py
+++ b/solution.py
@@ -252,8 +252,18 @@
 
         return gathered(part, lo, hi)
 
+    def partial(self, v, target, faces, x, inner, between):
+        face, py, my, pz, mz = faces
+        mid = v(x, x + 1)
+        across = py(x, x + 1) * roll_last(mid, -1) + my(x, x + 1) * roll_last(mid, 1)
+        above = next_of(mid, 1, lambda u: roll_rows(u, -1))
+        below = previous_of(mid, 1, lambda u: roll_rows(u, 1))
+        upright = pz(x, x + 1) * above + mz(x, x + 1) * below
+        return (target(x, x + 1) + face(between, between + 1) * v(inner, inner + 1)) + (across + upright)
+
     def before(self):
         old = self.olds[0]
+        self.near1, self.near2, self.near3 = [], [], []
         spans = self.ion_spans(old[0], 0, X)
         face = Span(spans[0].values[1:] + spans[0].values[:-1], 0)
         ion = ((face, *spans[1:]), self.ion_inverse(spans, face, 0, X), spans[0])
@@ -267,6 +277,12 @@
             self.total0.append(total)
             self.first0.append(first)
             self.mid1.append(self.last(old[f], self.target0[f], first, faces, inv, 2, X - 2))
+            near = []
+            for x, inner, between, opened in ((1, 2, 1, 0), (X - 2, X - 3, X - 3, X - 2)):
+                scale = take_new * inv(x, x + 1)
+                base = self.partial(first, self.target0[f], faces, x, inner, between)
+                near.append((base * scale - keep_old * old[f](x, x + 1), faces[0](opened, opened + 1) * scale))
+            self.near1.append(near)
         new = self.mid1
         self.spans1 = self.ion_spans(new[0], 2, X - 2)
         k = self.spans1[0]
@@ -280,6 +296,22 @@
             first = gathered(lambda a, b: self.sweep(new[f], self.target1[f], faces, a, b) * inv(a, b), 3, X - 3)
             self.first1.append(first)
             self.mid2.append(self.last(new[f], self.target1[f], first, faces, inv, 4, X - 4))
+            near = []
+            for x, inner, between, opened in ((2, 3, 2, 1), (X - 3, X - 4, X - 4, X - 3)):
+                base = self.partial(new[f], self.target1[f], faces, x, inner, between)
+                if f == 0:
+                    near.append((base * inv(x, x + 1), faces[0](opened, opened + 1) * inv(x, x + 1)))
+                else:
+                    rest = [part(x, x + 1) for part in faces[1:]]
+                    total = (1.0 + faces[0](between, between + 1)) + (rest[0] + rest[1]) + (rest[2] + rest[3])
+                    near.append((base, total))
+            self.near2.append(near)
+            near = []
+            for x, inner, between, opened in ((3, 4, 3, 2), (X - 4, X - 5, X - 5, X - 4)):
+                scale = take_new * inv(x, x + 1)
+                base = self.partial(first, self.target1[f], faces, x, inner, between)
+                near.append((base * scale - keep_old * new[f](x, x + 1), faces[0](opened, opened + 1) * scale))
+            self.near3.append(near)
 
     def after(self, trace):
         old = self.olds[0]
@@ -297,9 +329,12 @@
                 )
             first = Span(jnp.concatenate([ends[0], self.first0[f].values, ends[1]], axis=0), 0)
             target = Span(target, 0)
-            low = self.last(old[f], target, first, faces, inv, 0, 2)
-            high = self.last(old[f], target, first, faces, inv, X - 2, X)
-            news.append(joined(low, self.mid1[f], high))
+            (low, low_face), (high, high_face) = self.near1[f]
+            low = Span(low + low_face * ends[0], 1)
+            high = Span(high + high_face * ends[1], X - 2)
+            lowest = self.last(old[f], target, first, faces, inv, 0, 1)
+            highest = self.last(old[f], target, first, faces, inv, X - 1, X)
+            news.append(joined(lowest, low, self.mid1[f], high, highest))
             yield
         low, high = self.ion_spans(news[0], 0, 2), self.ion_spans(news[0], X - 2, X)
         spans = [joined(a, b, c) for a, b, c in zip(low, self.spans1, high)]
@@ -307,12 +342,21 @@
         face = Span(
             jnp.concatenate([k[1:3] + k[0:2], self.face1.values, k[X - 2 :] + k[X - 3 : X - 1]], axis=0), 0
         )
-        inv = joined(self.ion_inverse(spans, face, 0, 3), self.inv1, self.ion_inverse(spans, face, X - 3, X))
+        reached = [
+            inverse(self.near2[1][side][1] + face(between, between + 1)) for side, between in ((0, 1), (1, X - 3))
+        ]
+        inv = joined(
+            self.ion_inverse(spans, face, 0, 2),
+            Span(reached[0], 2),
+            self.inv1,
+            Span(reached[1], X - 3),
+            self.ion_inverse(spans, face, X - 2, X),
+        )
         yield
-        low, high = self.targets(1, news, 0, 2), self.targets(1, news, X - 2, X)
+        lows, highs = self.targets(1, news, 0, 2), self.targets(1, news, X - 2, X)
         ends = []
         for f, (faces, inv, k) in enumerate((self.heat, ((face, *spans[1:]), inv, spans[0]))):
-            target = joined(low[f], self.target1[f], high[f]).values
+            target = joined(lows[f], self.target1[f], highs[f]).values
             target = Span(
                 jnp.concatenate(
                     [
@@ -325,12 +369,26 @@
                 0,
             )
             part = lambda a, b: self.sweep(news[f], target, faces, a, b) * inv(a, b)
-            first = joined(gathered(part, 0, 3), self.first1[f], gathered(part, X - 3, X))
+            at2 = []
+            for side, x, beside, between in ((0, 2, 1, 1), (1, X - 3, X - 2, X - 3)):
+                base, other = self.near2[f][side]
+                given = news[f](beside, beside + 1)
+                if f == 0:
+                    at2.append(base + other * given)
+                else:
+                    at2.append((base + face(between, between + 1) * given) * inv(x, x + 1))
+            first = joined(
+                gathered(part, 0, 2), Span(at2[0], 2), self.first1[f], Span(at2[1], X - 3), gathered(part, X - 2, X)
+            )
+            (low, low_face), (high, high_face) = self.near3[f]
+            at3 = [low + low_face * at2[0], high + high_face * at2[1]]
             ends.append(
                 joined(
-                    self.last(news[f], target, first, faces, inv, 0, 4),
+                    self.last(news[f], target, first, faces, inv, 0, 3),
+                    Span(at3[0], 3),
                     self.mid2[f],
-                    self.last(news[f], target, first, faces, inv, X - 4, X),
+                    Span(at3[1], X - 4),
+                    self.last(news[f], target, first, faces, inv, X - 3, X),
                 )
             )
             yield

time: 9.63 us -> 9.61 us (level)
  no operation moved by 1% of the time
where the time goes in v7:
time: 9.61 us; the launch traced here: 9.48 us
  Pallas kernels  8.85 us (92%)
  between operations  0.64 us (7%)
    pallas_call x1, Pallas kernels, shards(): pl.pallas_call(functools.partial(kernel, n_gx, n_gy), out_shape=(jax.Shap...  8.08 us
    pallas_call x1, Pallas kernels, shards(): pl.pallas_call(write_out, out_shape=(pltpu.HBM((2, Z * X, C), jnp.float32...  0.76 us

profile of v7, /device:TPU:57, one launch (start us, length us, event | category | flops | bytes accessed | tf_op | source)
XLA Modules:
  0.0 9.5 jit_solution(4210322697565027284)
XLA Ops:
  0.6 8.1 %shard_map.59 = (f32[2,256,128]{2,1,0:T(8,128)S(1)}, f32[2,2,64,128]{3,2,1,0:T(8,128)S(1)}) custom-call(bf16[2,16,16,128]{3,2,1,0:T(8,128)(2,1)} %f_hbm.1, s32[16,128]{1,0:T(8,128)} %ph_hbm.1, s32[2,16,128]{2,1,0:T(8,128)} %el_hbm.1, f32[256,128]{1,0:T(8,128)} %bitcast.3), custom_call_target="tpu_custom_call" | custom-call | tf_op jit(solution)/shard_map/pallas_call | solution.py:724
  8.7 0.8 %shard_map.60 = (f32[2,256,128]{2,1,0:T(8,128)}, f32[2,2,64,128]{3,2,1,0:T(8,128)}) custom-call(f32[2,256,128]{2,1,0:T(8,128)S(1)} %get-tuple-element.6.f_ref, f32[2,2,64,128]{3,2,1,0:T(8,128)S(1)} %get-tuple-element.7.p_ref), custom_call_target="tpu_custom_call" | custom-call | tf_op jit(solution)/shard_map/pallas_call | solution.py:753

commit v8 on v7

--- a/solution.py
+++ b/solution.py
@@ -488,7 +488,7 @@
 
     barrier = pltpu.get_barrier_semaphore()
     expected = jnp.int32(0)
-    for offset in ALL:
+    for offset in SIDES_Y + CORNERS + SIDES_X:
 
         @pl.when(exists(offset))
         def _(offset=offset):

time: 9.61 us -> 9.61 us (level)
  no operation moved by 1% of the time
where the time goes in v8:
time: 9.61 us; the launch traced here: 9.48 us
  Pallas kernels  8.85 us (92%)
  between operations  0.64 us (7%)
    pallas_call x1, Pallas kernels, shards(): pl.pallas_call(functools.partial(kernel, n_gx, n_gy), out_shape=(jax.Shap...  8.08 us
    pallas_call x1, Pallas kernels, shards(): pl.pallas_call(write_out, out_shape=(pltpu.HBM((2, Z * X, C), jnp.float32...  0.76 us

profile of v8, /device:TPU:57, one launch (start us, length us, event | category | flops | bytes accessed | tf_op | source)
XLA Modules:
  0.0 9.5 jit_solution(8846165260799803562)
XLA Ops:
  0.6 8.1 %shard_map.59 = (f32[2,256,128]{2,1,0:T(8,128)S(1)}, f32[2,2,64,128]{3,2,1,0:T(8,128)S(1)}) custom-call(bf16[2,16,16,128]{3,2,1,0:T(8,128)(2,1)} %f_hbm.1, s32[16,128]{1,0:T(8,128)} %ph_hbm.1, s32[2,16,128]{2,1,0:T(8,128)} %el_hbm.1, f32[256,128]{1,0:T(8,128)} %bitcast.3), custom_call_target="tpu_custom_call" | custom-call | tf_op jit(solution)/shard_map/pallas_call | solution.py:724
  8.7 0.8 %shard_map.60 = (f32[2,256,128]{2,1,0:T(8,128)}, f32[2,2,64,128]{3,2,1,0:T(8,128)}) custom-call(f32[2,256,128]{2,1,0:T(8,128)S(1)} %get-tuple-element.6.f_ref, f32[2,2,64,128]{3,2,1,0:T(8,128)S(1)} %get-tuple-element.7.p_ref), custom_call_target="tpu_custom_call" | custom-call | tf_op jit(solution)/shard_map/pallas_call | solution.py:753

commit v9 on v6

--- a/solution.py
+++ b/solution.py
@@ -650,8 +650,8 @@
         pltpu.make_async_copy(f_ref, of_hbm, sem.at[0]),
         pltpu.make_async_copy(p_ref, op_hbm, sem.at[1]),
     ]
-    for copy in copies:
-        copy.start()
+    copies[0].start(priority=0)
+    copies[1].start(priority=1)
     for copy in copies:
         copy.wait()
 

time: 9.63 us -> 9.63 us (level)
  no operation moved by 1% of the time
where the time goes in v9:
time: 9.63 us; the launch traced here: 9.5 us
  Pallas kernels  8.86 us (92%)
  between operations  0.64 us (7%)
    pallas_call x1, Pallas kernels, shards(): pl.pallas_call(functools.partial(kernel, n_gx, n_gy), out_shape=(jax.Shap...  8.1 us
    pallas_call x1, Pallas kernels, shards(): pl.pallas_call(write_out, out_shape=(pltpu.HBM((2, Z * X, C), jnp.float32...  0.76 us

profile of v9, /device:TPU:57, one launch (start us, length us, event | category | flops | bytes accessed | tf_op | source)
XLA Modules:
  0.0 9.5 jit_solution(2129125579874189910)
XLA Ops:
  0.6 8.1 %shard_map.59 = (f32[2,256,128]{2,1,0:T(8,128)S(1)}, f32[2,2,64,128]{3,2,1,0:T(8,128)S(1)}) custom-call(bf16[2,16,16,128]{3,2,1,0:T(8,128)(2,1)} %f_hbm.1, s32[16,128]{1,0:T(8,128)} %ph_hbm.1, s32[2,16,128]{2,1,0:T(8,128)} %el_hbm.1, f32[256,128]{1,0:T(8,128)} %bitcast.3), custom_call_target="tpu_custom_call" | custom-call | tf_op jit(solution)/shard_map/pallas_call | solution.py:666
  8.7 0.8 %shard_map.60 = (f32[2,256,128]{2,1,0:T(8,128)}, f32[2,2,64,128]{3,2,1,0:T(8,128)}) custom-call(f32[2,256,128]{2,1,0:T(8,128)S(1)} %get-tuple-element.6.f_ref, f32[2,2,64,128]{3,2,1,0:T(8,128)S(1)} %get-tuple-element.7.p_ref), custom_call_target="tpu_custom_call" | custom-call | tf_op jit(solution)/shard_map/pallas_call | solution.py:695

commit v10 on v6

--- a/solution.py
+++ b/solution.py
@@ -430,7 +430,7 @@
 
     barrier = pltpu.get_barrier_semaphore()
     expected = jnp.int32(0)
-    for offset in ALL:
+    for offset in SIDES_Y + CORNERS + SIDES_X:
 
         @pl.when(exists(offset))
         def _(offset=offset):

time: 9.63 us -> 9.61 us (level)
  no operation moved by 1% of the time
where the time goes in v10:
time: 9.61 us; the launch traced here: 9.48 us
  Pallas kernels  8.85 us (92%)
  between operations  0.64 us (7%)
    pallas_call x1, Pallas kernels, shards(): pl.pallas_call(functools.partial(kernel, n_gx, n_gy), out_shape=(jax.Shap...  8.08 us
    pallas_call x1, Pallas kernels, shards(): pl.pallas_call(write_out, out_shape=(pltpu.HBM((2, Z * X, C), jnp.float32...  0.76 us

profile of v10, /device:TPU:57, one launch (start us, length us, event | category | flops | bytes accessed | tf_op | source)
XLA Modules:
  0.0 9.5 jit_solution(2878912164777667867)
XLA Ops:
  0.6 8.1 %shard_map.59 = (f32[2,256,128]{2,1,0:T(8,128)S(1)}, f32[2,2,64,128]{3,2,1,0:T(8,128)S(1)}) custom-call(bf16[2,16,16,128]{3,2,1,0:T(8,128)(2,1)} %f_hbm.1, s32[16,128]{1,0:T(8,128)} %ph_hbm.1, s32[2,16,128]{2,1,0:T(8,128)} %el_hbm.1, f32[256,128]{1,0:T(8,128)} %bitcast.3), custom_call_target="tpu_custom_call" | custom-call | tf_op jit(solution)/shard_map/pallas_call | solution.py:666
  8.7 0.8 %shard_map.60 = (f32[2,256,128]{2,1,0:T(8,128)}, f32[2,2,64,128]{3,2,1,0:T(8,128)}) custom-call(f32[2,256,128]{2,1,0:T(8,128)S(1)} %get-tuple-element.6.f_ref, f32[2,2,64,128]{3,2,1,0:T(8,128)S(1)} %get-tuple-element.7.p_ref), custom_call_target="tpu_custom_call" | custom-call | tf_op jit(solution)/shard_map/pallas_call | solution.py:695
